TPU v7x, 256 devices: a whole 4x4x8 slice. The times are simulated.
256 devices in a mesh: lat: 16 (over x, y_lo, core), lon: 16 (over z, y_hi).
Axes of the slice: x: 4, y: 4 (y_hi: 2, y_lo: 2; y = y_hi * 2 + y_lo), z: 8, core: 2. Of those that a mesh axis runs over, the one named last changes fastest.
Arguments:
- features: bfloat16 [256, 1440, 256], P('lat', 'lon'), may hold values from -6 to 6
- cotangent: bfloat16 [256, 1440, 256], P('lat', 'lon'), may hold values from -6 to 6
- basis: bfloat16 [256, 3, 3, 33], P('lat'), may hold values from -0.625 to 0.625
- support: int32 [256], P('lat'), may hold values from 1 to 16, as said below
- weight_one: bfloat16 [3, 256, 256], replicated, may hold values from -0.21875 to 0.21875
- weight_two: bfloat16 [3, 256, 256], replicated, may hold values from -0.21875 to 0.21875
Outputs:
- layer_out: bfloat16 [256, 1440, 256], P('lat', 'lon')
- grad_input: bfloat16 [256, 1440, 256], P('lat', 'lon')
- grad_one: float32 [3, 256, 256], replicated
- grad_two: float32 [3, 256, 256], replicated
Inputs may be any that keep to these rules, and one draw needn't show every extreme that they name: support[r] is how many cells on each side along longitude the filter of row r reaches; the first and the last row reach 16.
All inputs are finite; a program needn't handle non-finite values.
Results may differ from a plain program's by a relative error of at most 0.006.
The roundings to bfloat16 on the way count: a program that leaves them out, or rounds other values in their place, can miss the bound.
Values may be sent and summed in bfloat16 or wider, within the bound.
A program may use at most 64 MiB of HBM per device.

v0:
```python
import math

import jax
import jax.numpy as jnp
from jax import lax
from jax.sharding import PartitionSpec as P

HW = 16


def padded(cells, sides, width, closed):
    for axis, dim in sides:
        count = lax.axis_size(axis)
        ends = count if closed else count - 1
        head = lax.slice_in_dim(cells, 0, width, axis=dim)
        tail = lax.slice_in_dim(cells, cells.shape[dim] - width, cells.shape[dim], axis=dim)
        cells = jnp.concatenate(
            [
                lax.ppermute(tail, axis, [(i, (i + 1) % count) for i in range(ends)]),
                cells,
                lax.ppermute(head, axis, [((i + 1) % count, i) for i in range(ends)]),
            ],
            axis=dim,
        )
    return cells


def local(features, cotangent, basis, support, weight_one, weight_two):
    row_count, col_count, chan_count = features.shape
    basis_count = weight_one.shape[0]
    span_count = 2 * HW + 1
    pad_cols = col_count + 2 * HW
    scaling = 1.0 / math.sqrt(row_count * lax.axis_size("lat") * col_count * lax.axis_size("lon"))
    offset = jnp.abs(jnp.arange(span_count, dtype=jnp.int32) - HW)
    inside = offset[None, :] <= support[:, None]
    filtered = jnp.where(inside[:, None, None, :], basis, jnp.zeros_like(basis))
    off_idx = lax.broadcasted_iota(jnp.int32, (span_count, col_count, pad_cols), 0)
    out_idx = lax.broadcasted_iota(jnp.int32, (span_count, col_count, pad_cols), 1)
    pad_idx = lax.broadcasted_iota(jnp.int32, (span_count, col_count, pad_cols), 2)
    fwd_select = (pad_idx - out_idx == off_idx).astype(jnp.bfloat16)
    back_select = (out_idx + 2 * HW - pad_idx == off_idx).astype(jnp.bfloat16)
    band_fwd = jnp.einsum(
        "rkab,bjp->rkajp", filtered, fwd_select, preferred_element_type=jnp.float32
    ).astype(jnp.bfloat16)
    band_back = jnp.einsum(
        "rkab,bqp->rkaqp", filtered, back_select, preferred_element_type=jnp.float32
    ).astype(jnp.bfloat16)

    def stencil(field):
        lon_wide = padded(field, (("lon", 1),), HW, True)
        lat_wide = padded(lon_wide, (("lat", 0),), 1, False)
        stacked = jnp.stack(
            [lat_wide[0:row_count], lat_wide[1 : row_count + 1], lat_wide[2 : row_count + 2]]
        )
        return jnp.einsum(
            "rkajp,arpc->rjkc", band_fwd, stacked, preferred_element_type=jnp.float32
        ).astype(jnp.bfloat16)

    def spread(grad_wide):
        contrib = jnp.einsum(
            "rkaqp,rpkc->arqc", band_back, grad_wide, preferred_element_type=jnp.float32
        )
        total = contrib[1]
        total = total + jnp.pad(contrib[0][1:], ((0, 1), (0, 0), (0, 0)))
        total = total + jnp.pad(contrib[2][:-1], ((1, 0), (0, 0), (0, 0)))
        rim_rows = jnp.stack([contrib[0][0], contrib[2][row_count - 1]])
        spilled = padded(rim_rows, (("lat", 0),), 1, False)
        total = total + jnp.pad(spilled[0:1], ((0, row_count - 1), (0, 0), (0, 0)))
        total = total + jnp.pad(spilled[3:4], ((row_count - 1, 0), (0, 0), (0, 0)))
        return total

    def channel_mix(stacked, weight):
        flat = jnp.dot(
            stacked.reshape(-1, basis_count * chan_count),
            weight.reshape(basis_count * chan_count, chan_count),
            preferred_element_type=jnp.float32,
        )
        return flat.reshape(row_count, col_count, chan_count)

    def back_mix(grad_out, weight):
        lead_rows, lead_cols = (grad_out.shape[0], grad_out.shape[1])
        flat = jnp.dot(
            grad_out.reshape(-1, chan_count),
            weight.reshape(basis_count * chan_count, chan_count).T,
            preferred_element_type=jnp.float32,
        )
        return flat.astype(jnp.bfloat16).reshape(lead_rows, lead_cols, basis_count, chan_count)

    def weight_grad(stacked, grad_out):
        summed = lax.dot_general(
            stacked.reshape(-1, basis_count * chan_count),
            grad_out.reshape(-1, chan_count),
            (((0,), (0,)), ((), ())),
            preferred_element_type=jnp.float32,
        )
        return (summed * scaling).reshape(basis_count, chan_count, chan_count)

    def grad_margin(grad_out, weight):
        grad_basis = back_mix(grad_out, weight)
        return padded(grad_basis, (("lon", 1),), HW, True)

    y_one = stencil(features)
    z_one = channel_mix(y_one, weight_one)
    hidden = jax.nn.silu(z_one).astype(jnp.bfloat16)
    y_two = stencil(hidden)
    layer_out = channel_mix(y_two, weight_two).astype(jnp.bfloat16)
    grad_two = weight_grad(y_two, cotangent)
    wide_two = grad_margin(cotangent, weight_two)
    sigma = jax.nn.sigmoid(z_one)
    dz_one = (spread(wide_two) * sigma * (1.0 + z_one * (1.0 - sigma))).astype(jnp.bfloat16)
    grad_one = weight_grad(y_one, dz_one)
    wide_one = grad_margin(dz_one, weight_one)
    grad_input = spread(wide_one).astype(jnp.bfloat16)
    grad_one, grad_two = lax.psum((grad_one, grad_two), ("lat", "lon"))
    return (layer_out, grad_input, grad_one, grad_two)


def solution(mesh):
    placed = (
        P("lat", "lon", None),
        P("lat", "lon", None),
        P("lat", None, None, None),
        P("lat"),
        P(),
        P(),
    )
    return jax.shard_map(
        local,
        mesh=mesh,
        in_specs=placed,
        out_specs=(P("lat", "lon", None), P("lat", "lon", None), P(), P()),
        check_vma=False,
    )
```

profile of v0, /device:TPU:1, one launch (start us, length us, event | category | flops | bytes accessed | tf_op | source)
XLA Modules:
  0.0 379.0 jit_solution(6003215240322763370)
XLA Ops:
  10.3 3.7 collective-permute-start
  14.1 5.3 %collective-permute-start.1 = (bf16[16,16,256]{2,1,0:T(8,128)(2,1)}, bf16[16,16,256]{2,1,0:T(8,128)(2,1)}, u32[]{:S(2)}, u32[]{:S(2)}) collective-permute-start(bf16[16,16,256]{2,1,0:T(8,128)(2,1)} %get-tuple-element.41), channel_id=1, source_target_pairs={{1,0},{2,1},{3,2},{4,3},{5,4},{6,5},{7,6},{8,7},{9,8},{10,9},{11,1... | collective-permute-start | bytes 393224 | tf_op jit(solution)/shard_map/ppermute | solution.py:21
  22.8 5.6 %reshape.88 = bf16[16,90,3,256]{3,2,1,0:T(4,128)(2,1)S(1)} reshape(bf16[1440,768]{1,0:T(8,128)(2,1)} %convolution_convert_fusion.1) | data formatting | bytes 4423680 | tf_op jit(solution)/shard_map/reshape | solution.py:87
  29.2 5.1 %collective-permute-start.9 = (bf16[16,16,3,256]{3,1,2,0:T(8,128)(2,1)S(1)}, bf16[16,16,3,256]{3,1,2,0:T(8,128)(2,1)S(1)}, u32[]{:S(2)}, u32[]{:S(2)}) collective-permute-start(bf16[16,16,3,256]{3,1,2,0:T(8,128)(2,1)S(1)} %get-tuple-element.25), channel_id=1, source_target_pairs={{1,0},{2,1},{3,2},{4,3},{5,4},{6,5},{7,6},{8,7},{9,8},{10,9},{11,1... | collective-permute-start | bytes 1179656 | tf_op jit(solution)/shard_map/ppermute | solution.py:21
  36.7 3.7 collective-permute-start.2
  43.5 4.0 %collective-permute-done.2 = bf16[1,122,256]{2,1,0:T(8,128)(2,1)S(1)} collective-permute-done((bf16[1,122,256]{2,1,0:T(8,128)(2,1)S(1)}, bf16[1,122,256]{2,1,0:T(8,128)(2,1)S(1)}, u32[]{:S(2)}, u32[]{:S(2)}) %collective-permute-start.2) | collective-permute-done | bytes 62496 | tf_op jit(solution)/shard_map/ppermute | solution.py:19
  50.1 2.3 fusion.21
  56.4 2.6 fusion.26
  59.0 3.7 collective-permute-start.10
  65.0 3.7 collective-permute-done.11
  70.8 2.6 collective-permute-start.4
  73.4 2.5 collective-permute-start.5
  76.0 3.3 convolution_multiply_fusion.1
  79.3 2.2 convolution_convert_fusion
  81.5 5.6 %reshape.91 = bf16[16,90,3,256]{3,2,1,0:T(4,128)(2,1)S(1)} reshape(bf16[1440,768]{1,0:T(8,128)(2,1)} %convolution_convert_fusion) | data formatting | bytes 4423680 | tf_op jit(solution)/shard_map/reshape | solution.py:87
  89.4 2.3 collective-permute-start.6
  95.1 4.7 %collective-permute-start.13 = (bf16[16,16,3,256]{3,1,2,0:T(8,128)(2,1)S(1)}, bf16[16,16,3,256]{3,1,2,0:T(8,128)(2,1)}, u32[]{:S(2)}, u32[]{:S(2)}) collective-permute-start(bf16[16,16,3,256]{3,1,2,0:T(8,128)(2,1)S(1)} %get-tuple-element.23), channel_id=1, source_target_pairs={{1,0},{2,1},{3,2},{4,3},{5,4},{6,5},{7,6},{8,7},{9,8},{10,9},{11,1... | collective-permute-start | bytes 1179656 | tf_op jit(solution)/shard_map/ppermute | solution.py:21
  101.7 2.3 fusion.22
  110.4 3.0 collective-permute-done.12
  113.4 2.8 collective-permute-done.13
  116.2 3.6 fusion.23
  119.8 2.5 collective-permute-start.14
  124.6 4.2 %collective-permute-done.15 = f32[1,90,256]{2,1,0:T(8,128)S(1)} collective-permute-done((f32[1,90,256]{2,1,0:T(8,128)S(1)}, f32[1,90,256]{2,1,0:T(8,128)S(1)}, u32[]{:S(2)}, u32[]{:S(2)}) %collective-permute-start.15) | collective-permute-done | bytes 92192 | tf_op jit(solution)/shard_map/ppermute | solution.py:21
  130.6 237.4 %all-reduce.11.cloned.1.call-done = (f32[3,256,256]{2,1,0:T(8,128)}, f32[3,256,256]{2,1,0:T(8,128)}) async-done(((f32[3,256,256]{2,1,0:T(8,128)}, f32[3,256,256]{2,1,0:T(8,128)}), (f32[3,256,256]{2,1,0:T(8,128)}, f32[3,256,256]{2,1,0:T(8,128)})) %all-reduce.11.cloned.1.call-update) | async-done | bytes 1572880 | tf_op jit(solution)/shard_map/psum | solution.py:114
  (93 shorter events, 45.8 us)
Async XLA Ops:
  7.2 61.5 %copy-start = (bf16[3,256,256]{2,1,0:T(8,128)(2,1)S(1)}, bf16[3,256,256]{2,1,0:T(8,128)(2,1)}, u32[]{:S(2)}) copy-start(bf16[3,256,256]{2,1,0:T(8,128)(2,1)} %param.10) | copy-start | bytes 1179652
  7.2 12.2 %copy-start.13 = (bf16[16,90,256]{2,0,1:T(8,128)(2,1)S(1)}, bf16[16,90,256]{2,0,1:T(8,128)(2,1)}, u32[]{:S(2)}) copy-start(bf16[16,90,256]{2,0,1:T(8,128)(2,1)} %param.7) | copy-start | bytes 2211844
  7.2 13.5 %copy-start.14 = (bf16[3,256,256]{2,1,0:T(8,128)(2,1)S(1)}, bf16[3,256,256]{2,1,0:T(8,128)(2,1)}, u32[]{:S(2)}) copy-start(bf16[3,256,256]{2,1,0:T(8,128)(2,1)} %param.11) | copy-start | bytes 1179652
  7.2 360.8 %all-reduce.11.cloned.1.call-start = ((), (), s32[]{:S(2)}) async-start(), calls=%async_computation | async-start | bytes 3145728 | tf_op jit(solution)/shard_map/psum | solution.py:114
  10.3 25.1 %collective-permute-start = (bf16[16,16,256]{2,1,0:T(8,128)(2,1)}, bf16[16,16,256]{2,1,0:T(8,128)(2,1)S(1)}, u32[]{:S(2)}, u32[]{:S(2)}) collective-permute-start(bf16[16,16,256]{2,1,0:T(8,128)(2,1)} %get-tuple-element.40), channel_id=1, source_target_pairs={{0,1},{1,2},{2,3},{3,4},{4,5},{5,6},{6,7},{7,8},{8,9},{9,10},{10,1... | collective-permute-start | bytes 393224 | tf_op jit(solution)/shard_map/ppermute | solution.py:19
  14.1 21.4 %collective-permute-start.1 = (bf16[16,16,256]{2,1,0:T(8,128)(2,1)}, bf16[16,16,256]{2,1,0:T(8,128)(2,1)}, u32[]{:S(2)}, u32[]{:S(2)}) collective-permute-start(bf16[16,16,256]{2,1,0:T(8,128)(2,1)} %get-tuple-element.41), channel_id=1, source_target_pairs={{1,0},{2,1},{3,2},{4,3},{5,4},{6,5},{7,6},{8,7},{9,8},{10,9},{11,1... | collective-permute-start | bytes 393224 | tf_op jit(solution)/shard_map/ppermute | solution.py:21
  29.1 27.3 %collective-permute-start.8 = (bf16[16,16,3,256]{3,1,2,0:T(8,128)(2,1)S(1)}, bf16[16,16,3,256]{3,1,2,0:T(8,128)(2,1)S(1)}, u32[]{:S(2)}, u32[]{:S(2)}) collective-permute-start(bf16[16,16,3,256]{3,1,2,0:T(8,128)(2,1)S(1)} %get-tuple-element.24), channel_id=1, source_target_pairs={{0,1},{1,2},{2,3},{3,4},{4,5},{5,6},{6,7},{7,8},{8,9},{9,10},{10,1... | collective-permute-start | bytes 1179656 | tf_op jit(solution)/shard_map/ppermute | solution.py:19
  29.2 27.2 %collective-permute-start.9 = (bf16[16,16,3,256]{3,1,2,0:T(8,128)(2,1)S(1)}, bf16[16,16,3,256]{3,1,2,0:T(8,128)(2,1)S(1)}, u32[]{:S(2)}, u32[]{:S(2)}) collective-permute-start(bf16[16,16,3,256]{3,1,2,0:T(8,128)(2,1)S(1)} %get-tuple-element.25), channel_id=1, source_target_pairs={{1,0},{2,1},{3,2},{4,3},{5,4},{6,5},{7,6},{8,7},{9,8},{10,9},{11,1... | collective-permute-start | bytes 1179656 | tf_op jit(solution)/shard_map/ppermute | solution.py:21
  35.4 20.9 %copy-start.6 = (bf16[16,3,3,90,122]{4,0,3,2,1:T(8,128)(2,1)}, bf16[16,3,3,90,122]{4,0,3,2,1:T(8,128)(2,1)S(1)}, u32[]{:S(2)}) copy-start(bf16[16,3,3,90,122]{4,0,3,2,1:T(8,128)(2,1)S(1)} %convolution_convert_fusion.2) | copy-start | bytes 9486724
  36.7 10.8 %collective-permute-start.2 = (bf16[1,122,256]{2,1,0:T(8,128)(2,1)S(1)}, bf16[1,122,256]{2,1,0:T(8,128)(2,1)S(1)}, u32[]{:S(2)}, u32[]{:S(2)}) collective-permute-start(bf16[1,122,256]{2,1,0:T(8,128)(2,1)S(1)} %get-tuple-element.36), channel_id=1, source_target_pairs={{0,16},{16,32},{32,48},{48,64},{64,80},{80,96},{96,112},{112,128},... | collective-permute-start | bytes 187400 | tf_op jit(solution)/shard_map/ppermute | solution.py:19
  40.4 8.0 %collective-permute-start.3 = (bf16[1,122,256]{2,1,0:T(8,128)(2,1)S(1)}, bf16[1,122,256]{2,1,0:T(8,128)(2,1)S(1)}, u32[]{:S(2)}, u32[]{:S(2)}) collective-permute-start(bf16[1,122,256]{2,1,0:T(8,128)(2,1)S(1)} %get-tuple-element.37), channel_id=1, source_target_pairs={{16,0},{32,16},{48,32},{64,48},{80,64},{96,80},{112,96},{128,112},... | collective-permute-start | bytes 187400 | tf_op jit(solution)/shard_map/ppermute | solution.py:21
  59.0 5.9 %collective-permute-start.10 = (f32[1,90,256]{2,1,0:T(8,128)S(1)}, f32[1,90,256]{2,1,0:T(8,128)S(1)}, u32[]{:S(2)}, u32[]{:S(2)}) collective-permute-start(f32[1,90,256]{2,1,0:T(8,128)S(1)} %get-tuple-element.20), channel_id=1, source_target_pairs={{0,16},{16,32},{32,48},{48,64},{64,80},{80,96},{96,112},{112,128},... | collective-permute-start | bytes 276488 | tf_op jit(solution)/shard_map/ppermute | solution.py:19
  62.7 5.9 %collective-permute-start.11 = (f32[1,90,256]{2,1,0:T(8,128)S(1)}, f32[1,90,256]{2,1,0:T(8,128)S(1)}, u32[]{:S(2)}, u32[]{:S(2)}) collective-permute-start(f32[1,90,256]{2,1,0:T(8,128)S(1)} %get-tuple-element.21), channel_id=1, source_target_pairs={{16,0},{32,16},{48,32},{64,48},{80,64},{96,80},{112,96},{128,112},... | collective-permute-start | bytes 276488 | tf_op jit(solution)/shard_map/ppermute | solution.py:21
  69.9 9.4 %copy-start.7 = (bf16[16,90,256]{2,1,0:T(8,128)(2,1)}, bf16[16,90,256]{2,1,0:T(8,128)(2,1)S(1)}, u32[]{:S(2)}) copy-start(bf16[16,90,256]{2,1,0:T(8,128)(2,1)S(1)} %get-tuple-element.27) | copy-start | bytes 2211844
  70.8 16.7 %collective-permute-start.4 = (bf16[16,16,256]{2,1,0:T(8,128)(2,1)}, bf16[16,16,256]{2,1,0:T(8,128)(2,1)S(1)}, u32[]{:S(2)}, u32[]{:S(2)}) collective-permute-start(bf16[16,16,256]{2,1,0:T(8,128)(2,1)} %get-tuple-element.38), channel_id=1, source_target_pairs={{0,1},{1,2},{2,3},{3,4},{4,5},{5,6},{6,7},{7,8},{8,9},{9,10},{10,1... | collective-permute-start | bytes 393224 | tf_op jit(solution)/shard_map/ppermute | solution.py:19
  73.4 14.2 %collective-permute-start.5 = (bf16[16,16,256]{2,1,0:T(8,128)(2,1)}, bf16[16,16,256]{2,1,0:T(8,128)(2,1)}, u32[]{:S(2)}, u32[]{:S(2)}) collective-permute-start(bf16[16,16,256]{2,1,0:T(8,128)(2,1)} %get-tuple-element.39), channel_id=1, source_target_pairs={{1,0},{2,1},{3,2},{4,3},{5,4},{6,5},{7,6},{8,7},{9,8},{10,9},{11,1... | collective-permute-start | bytes 393224 | tf_op jit(solution)/shard_map/ppermute | solution.py:21
  87.6 14.1 %copy-start.9 = (bf16[16,90,3,256]{3,1,2,0:T(8,128)(2,1)}, bf16[16,90,3,256]{3,1,2,0:T(8,128)(2,1)S(1)}, u32[]{:S(2)}) copy-start(bf16[16,90,3,256]{3,1,2,0:T(8,128)(2,1)S(1)} %copy.47) | copy-start | bytes 6635524
  89.4 10.4 %collective-permute-start.6 = (bf16[1,122,256]{2,1,0:T(8,128)(2,1)S(1)}, bf16[1,122,256]{2,1,0:T(8,128)(2,1)S(1)}, u32[]{:S(2)}, u32[]{:S(2)}) collective-permute-start(bf16[1,122,256]{2,1,0:T(8,128)(2,1)S(1)} %get-tuple-element.31), channel_id=1, source_target_pairs={{0,16},{16,32},{32,48},{48,64},{64,80},{80,96},{96,112},{112,128},... | collective-permute-start | bytes 187400 | tf_op jit(solution)/shard_map/ppermute | solution.py:19
  91.8 8.0 %collective-permute-start.7 = (bf16[1,122,256]{2,1,0:T(8,128)(2,1)S(1)}, bf16[1,122,256]{2,1,0:T(8,128)(2,1)S(1)}, u32[]{:S(2)}, u32[]{:S(2)}) collective-permute-start(bf16[1,122,256]{2,1,0:T(8,128)(2,1)S(1)} %get-tuple-element.32), channel_id=1, source_target_pairs={{16,0},{32,16},{48,32},{64,48},{80,64},{96,80},{112,96},{128,112},... | collective-permute-start | bytes 187400 | tf_op jit(solution)/shard_map/ppermute | solution.py:21
  94.7 18.6 %collective-permute-start.12 = (bf16[16,16,3,256]{3,1,2,0:T(8,128)(2,1)}, bf16[16,16,3,256]{3,1,2,0:T(8,128)(2,1)}, u32[]{:S(2)}, u32[]{:S(2)}) collective-permute-start(bf16[16,16,3,256]{3,1,2,0:T(8,128)(2,1)} %get-tuple-element.22), channel_id=1, source_target_pairs={{0,1},{1,2},{2,3},{3,4},{4,5},{5,6},{6,7},{7,8},{8,9},{9,10},{10,1... | collective-permute-start | bytes 1179656 | tf_op jit(solution)/shard_map/ppermute | solution.py:19
  95.1 21.0 %collective-permute-start.13 = (bf16[16,16,3,256]{3,1,2,0:T(8,128)(2,1)S(1)}, bf16[16,16,3,256]{3,1,2,0:T(8,128)(2,1)}, u32[]{:S(2)}, u32[]{:S(2)}) collective-permute-start(bf16[16,16,3,256]{3,1,2,0:T(8,128)(2,1)S(1)} %get-tuple-element.23), channel_id=1, source_target_pairs={{1,0},{2,1},{3,2},{4,3},{5,4},{6,5},{7,6},{8,7},{9,8},{10,9},{11,1... | collective-permute-start | bytes 1179656 | tf_op jit(solution)/shard_map/ppermute | solution.py:21
  119.8 4.8 %collective-permute-start.14 = (f32[1,90,256]{2,1,0:T(8,128)S(1)}, f32[1,90,256]{2,1,0:T(8,128)S(1)}, u32[]{:S(2)}, u32[]{:S(2)}) collective-permute-start(f32[1,90,256]{2,1,0:T(8,128)S(1)} %get-tuple-element.16), channel_id=1, source_target_pairs={{0,16},{16,32},{32,48},{48,64},{64,80},{80,96},{96,112},{112,128},... | collective-permute-start | bytes 276488 | tf_op jit(solution)/shard_map/ppermute | solution.py:19
  122.3 6.5 %collective-permute-start.15 = (f32[1,90,256]{2,1,0:T(8,128)S(1)}, f32[1,90,256]{2,1,0:T(8,128)S(1)}, u32[]{:S(2)}, u32[]{:S(2)}) collective-permute-start(f32[1,90,256]{2,1,0:T(8,128)S(1)} %get-tuple-element.17), channel_id=1, source_target_pairs={{16,0},{32,16},{48,32},{64,48},{80,64},{96,80},{112,96},{128,112},... | collective-permute-start | bytes 276488 | tf_op jit(solution)/shard_map/ppermute | solution.py:21
  128.8 243.4 %copy-start.1 = (bf16[3,256,256]{2,1,0:T(8,128)(2,1)S(1)}, bf16[3,256,256]{2,1,0:T(8,128)(2,1)}, u32[]{:S(2)}) copy-start(bf16[3,256,256]{2,1,0:T(8,128)(2,1)} %param.10) | copy-start | bytes 1179652
  (11 other events, 43.4 us)
Sparse Core Ops, SparseCore 0:
  110.5 257.4 all-reduce.10
where the time goes:
time: 381 us; the launch traced here: 379 us
  waiting for transfers between devices  256 us (67%)
  starting transfers between devices  44.6 us (12%)
  local copies, waits for them, and re-layouts  32.9 us (9%)
  matrix products  24.4 us (6%)
  between operations  14.5 us (4%)
  other arithmetic  6.64 us (2%)
    psum x1, waiting for transfers between devices, local(): grad_one, grad_two = lax.psum((grad_one, grad_two), ('lat', 'lon'))  237 us
    ppermute x8, starting transfers between devices, padded(): lax.ppermute(head, axis, [((i + 1) % count, i) for i in range(ends)])  25.5 us
    ppermute x8, starting transfers between devices, padded(): lax.ppermute(tail, axis, [(i, (i + 1) % count) for i in range(ends)])  19.1 us
    unnamed x44, local copies, waits for them, and re-layouts  13.4 us
    reshape x4, local copies, waits for them, and re-layouts, back_mix(): flat.astype(jnp.bfloat16)  12 us
    ppermute x8, waiting for transfers between devices, padded(): lax.ppermute(head, axis, [((i + 1) % count, i) for i in range(ends)])  11.6 us
  transfers between devices with their start and end apart: 17, of which 7 were waited for; matrix products, arithmetic and copies ran while one was open for 13% of the time, Pallas kernels for 0%

commit v1 on v0

v1 whole, which is shorter than its diff:
```python
import functools
import math

import jax
import jax.numpy as jnp
from jax import lax
from jax.experimental import pallas as pl
from jax.experimental.pallas import tpu as pltpu
from jax.sharding import PartitionSpec as P

HW = 16
WIDE = 128
MESH = pl.DeviceIdType.MESH
BF = jnp.bfloat16
F32 = jnp.float32
NT = (((1,), (1,)), ((), ()))
TN = (((0,), (0,)), ((), ()))


def dot(a, b, dims=(((1,), (0,)), ((), ()))):
    return lax.dot_general(a, b, dims, preferred_element_type=F32)


def kernel(
    dims,
    f_ref,
    c_ref,
    tf_ref,
    tb_ref,
    w1_ref,
    w2_ref,
    out_ref,
    gin_ref,
    g1_ref,
    g2_ref,
    ext_f,
    ext_c,
    ext_h,
    ext_d,
    tails,
    taps,
    band,
    back,
    y1,
    y2,
    dsig,
    dy,
    part,
    p32,
    gb,
    r1,
    sb,
    r2,
    s3,
    r3,
    r4,
    rowtmp,
    gfull,
    halo_snd,
    halo_rcv,
    tap_snd,
    tap_rcv,
    core_snd,
    core_rcv,
    x_snd,
    x_rcv,
    yz_snd,
    yz_rcv,
):
    nx, nyl, nz, nyh, rows, cols, chans, basis, scaling = dims
    own = -(-cols // 16) * 16
    right = own
    left = WIDE - HW
    nlat, nlon = nx * nyl * 2, nz * nyh
    ny = nyl * nyh
    nyz = nz * ny
    blk = 4
    nblk = rows // blk

    lat = lax.axis_index("lat")
    lon = lax.axis_index("lon")
    my_x = lat // (nyl * 2)
    my_core = lat % 2
    my_y = (lon % nyh) * nyl + (lat // 2) % nyl
    my_z = lon // nyh
    me_yz = my_z * ny + my_y
    north, south = (lat + nlat - 1) % nlat, (lat + 1) % nlat
    west, east = (lon + nlon - 1) % nlon, (lon + 1) % nlon

    def yz_device(idx):
        z, y = idx // ny, idx % ny
        return my_x * (nyl * 2) + (y % nyl) * 2 + my_core, z * nyh + y // nyl

    def x_device(x):
        return x * (nyl * 2) + lat % (nyl * 2), lon

    partner = (lat + 1 - 2 * my_core, lon)
    around = [
        (lat, east),
        (lat, west),
        (south, lon),
        (north, lon),
        (south, east),
        (north, east),
        (south, west),
        (north, west),
    ]

    barrier = pltpu.get_barrier_semaphore()

    def greet(device):
        pl.semaphore_signal(barrier, inc=1, device_id=device, device_id_type=MESH)

    for device in around:
        greet(device)
    greet(partner)
    for d in range(1, nx):
        greet(x_device((my_x + d) % nx))

    def greet_yz(d, carry):
        greet(yz_device((me_yz + d) % nyz))
        return carry

    lax.fori_loop(1, nyz, greet_yz, 0)

    def put_tail(field, r, value):
        tails[field, r] = value[cols - HW : cols].astype(BF)

    def stage(field, src, ext):
        def body(r, carry):
            value = src[r].astype(F32)
            wide = jnp.concatenate([value, jnp.zeros((own - cols, chans), F32)], axis=0)
            ext[r + 1, pl.ds(0, own)] = wide.astype(BF)
            put_tail(field, r, value)
            return carry

        lax.fori_loop(0, rows, body, 0)

    def halo(field, ext):
        tail = tails.at[field]
        body = pl.ds(1, rows)
        moves = [
            (tail, ext.at[body, pl.ds(left, HW)]),
            (ext.at[body, pl.ds(0, HW)], ext.at[body, pl.ds(right, HW)]),
            (ext.at[rows, pl.ds(0, own)], ext.at[0, pl.ds(0, own)]),
            (ext.at[1, pl.ds(0, own)], ext.at[rows + 1, pl.ds(0, own)]),
            (tail.at[rows - 1], ext.at[0, pl.ds(left, HW)]),
            (tail.at[0], ext.at[rows + 1, pl.ds(left, HW)]),
            (ext.at[rows, pl.ds(0, HW)], ext.at[0, pl.ds(right, HW)]),
            (ext.at[1, pl.ds(0, HW)], ext.at[rows + 1, pl.ds(right, HW)]),
        ]
        return [
            pltpu.make_async_remote_copy(
                src_ref=src,
                dst_ref=dst,
                send_sem=halo_snd.at[field, i],
                recv_sem=halo_rcv.at[field, i],
                device_id=around[i],
                device_id_type=MESH,
            )
            for i, (src, dst) in enumerate(moves)
        ]

    def tap_copies():
        return [
            pltpu.make_async_remote_copy(
                src_ref=taps.at[src],
                dst_ref=taps.at[dst],
                send_sem=tap_snd.at[i],
                recv_sem=tap_rcv.at[i],
                device_id=device,
                device_id_type=MESH,
            )
            for i, (src, dst, device) in enumerate(
                [(rows, 0, (south, lon)), (1, rows + 1, (north, lon))]
            )
        ]

    def start(copies):
        for copy in copies:
            copy.start()

    def arrive(copies):
        for copy in copies:
            copy.wait_recv()

    stage(0, f_ref, ext_f)
    stage(1, c_ref, ext_c)
    taps[pl.ds(1, rows)] = tb_ref[...]
    pl.semaphore_wait(barrier, len(around) + 1 + (nx - 1) + (nyz - 1))
    start(halo(0, ext_f))
    start(tap_copies())
    start(halo(1, ext_c))

    low = own - 24
    lane = lax.broadcasted_iota(jnp.int32, (24, WIDE), 1)
    cell = lax.broadcasted_iota(jnp.int32, (24, WIDE), 0) + low
    valid = cell < cols
    plain = valid & ((lane < cols) | (lane >= left))
    moved = valid & (lane >= right) & (lane < left)
    gap = own - cols

    def toeplitz(tap):
        wide = jnp.broadcast_to(tap, (own, WIDE))
        t = pltpu.roll(wide, 0, 1, stride=1, stride_axis=0)
        t6 = pltpu.roll(wide[:24], low + gap, 1, stride=1, stride_axis=0)
        bottom = jnp.where(moved, t6, jnp.where(plain, t[low:], 0.0))
        return jnp.concatenate([t[:low], bottom], axis=0).astype(BF)

    def build_fwd(r, carry):
        for k in range(basis):
            for a in range(3):
                tap = tf_ref[r, pl.ds(k * 3 + a, 1), :]
                band[r, pl.ds(k * own, own), pl.ds(a * WIDE, WIDE)] = toeplitz(tap)
        return carry

    lax.fori_loop(0, rows, build_fwd, 0)

    def build_back(i, sides=(0, 1, 2), keep=None):
        for k in range(basis):
            for a in sides:
                tap = taps[i, pl.ds(k * 3 + a, 1), :]
                if keep is not None:
                    tap = jnp.where(keep, tap, 0.0)
                back[i, pl.ds(a * own, own), pl.ds(k * WIDE, WIDE)] = toeplitz(tap)

    def build_back_loop(i, carry):
        build_back(i)
        return carry

    lax.fori_loop(1, rows + 1, build_back_loop, 0)

    def stencil(ext, y, r):
        x = ext[pl.ds(r, 3)].reshape(3 * WIDE, chans)
        t = dot(band[r], x).astype(BF)
        for k in range(basis):
            y[r, :, pl.ds(k * chans, chans)] = t[k * own : (k + 1) * own]

    def mix(y, w_ref, r0):
        flat = y[pl.ds(r0, blk)].reshape(blk * own, basis * chans)
        return dot(flat, w_ref[...].reshape(basis * chans, chans))

    arrive(halo(0, ext_f))

    def first(b, carry):
        r0 = b * blk
        for i in range(blk):
            stencil(ext_f, y1, r0 + i)
        z = mix(y1, w1_ref, r0)
        sigma = jax.nn.sigmoid(z)
        dsig[pl.ds(r0, blk)] = (sigma * (1.0 + z * (1.0 - sigma))).reshape(blk, own, chans)
        hidden = (z * sigma).reshape(blk, own, chans)
        ext_h[pl.ds(r0 + 1, blk), pl.ds(0, own)] = hidden.astype(BF)
        for i in range(blk):
            put_tail(2, r0 + i, hidden[i])
        return carry

    lax.fori_loop(0, nblk, first, 0)
    start(halo(2, ext_h))

    def spread_rows(ext, w_ref, i0, count):
        flat = ext[pl.ds(i0, count)].reshape(count * WIDE, chans)
        for k in range(basis):
            d = dot(flat, w_ref[k], NT).astype(BF)
            dy[pl.ds(i0, count), k] = d.reshape(count, WIDE, chans)

    def spread(ext, w_ref):
        def body(b, carry):
            i0 = 1 + b * blk
            spread_rows(ext, w_ref, i0, blk)
            for i in range(blk):
                u = dy[i0 + i].reshape(basis * WIDE, chans)
                part[i0 + i] = dot(back[i0 + i], u).reshape(3, own, chans)
            return carry

        lax.fori_loop(0, nblk, body, 0)
        for i, a in ((0, 2), (rows + 1, 0)):
            spread_rows(ext, w_ref, i, 1)
            u = dy[i].reshape(basis * WIDE, chans)
            part[i, a] = dot(back[i, pl.ds(a * own, own)], u)

    def gathered(r0):
        return (
            part[pl.ds(r0, blk), 2] + part[pl.ds(r0 + 1, blk), 1] + part[pl.ds(r0 + 2, blk), 0]
        )

    arrive(tap_copies())
    build_back(0, (2,), lat > 0)
    build_back(rows + 1, (0,), lat < nlat - 1)
    arrive(halo(1, ext_c))
    spread(ext_c, w2_ref)

    def activation(b, carry):
        r0 = b * blk
        dz = gathered(r0) * dsig[pl.ds(r0, blk)]
        ext_d[pl.ds(r0 + 1, blk), pl.ds(0, own)] = dz.astype(BF)
        for i in range(blk):
            put_tail(3, r0 + i, dz[i])
        return carry

    lax.fori_loop(0, nblk, activation, 0)
    start(halo(3, ext_d))

    chunk = basis * chans // (2 * nx)
    piece = chunk // nyz

    def weight_grad(g, y, ext):
        flat = y[...].reshape(rows * own, basis * chans)
        grad = ext[pl.ds(1, rows), pl.ds(0, own)].reshape(rows * own, chans)
        p32[g] = dot(flat, grad, TN).reshape(2, nx, chunk, chans)
        gb[g] = p32[g, 1 - my_core].astype(BF)

    def remote(src, dst, snd, rcv, device):
        return pltpu.make_async_remote_copy(
            src_ref=src,
            dst_ref=dst,
            send_sem=snd,
            recv_sem=rcv,
            device_id=device,
            device_id_type=MESH,
        )

    def core_scatter(g):
        return [remote(gb.at[g], r1.at[g], core_snd.at[g, 0], core_rcv.at[g, 0], partner)]

    def x_scatter(g):
        return [
            remote(
                sb.at[g, (my_x + d) % nx],
                r2.at[g, d - 1],
                x_snd.at[g, 0, d],
                x_rcv.at[g, 0, d],
                x_device((my_x + d) % nx),
            )
            for d in range(1, nx)
        ]

    def yz_scatter(g, d):
        peer = (me_yz + d) % nyz
        return remote(
            s3.at[g, peer],
            r3.at[g, me_yz],
            yz_snd.at[g, 0, d],
            yz_rcv.at[g, 0, d],
            yz_device(peer),
        )

    def yz_gather(g, d):
        peer = (me_yz + d) % nyz
        return remote(
            r4.at[g, me_yz],
            r4.at[g, me_yz],
            yz_snd.at[g, 1, d],
            yz_rcv.at[g, 1, d],
            yz_device(peer),
        )

    def x_gather(g):
        return [
            remote(
                gfull.at[g, my_core, my_x],
                gfull.at[g, my_core, my_x],
                x_snd.at[g, 1, d],
                x_rcv.at[g, 1, d],
                x_device((my_x + d) % nx),
            )
            for d in range(1, nx)
        ]

    def core_gather(g):
        return [
            remote(
                gfull.at[g, my_core],
                gfull.at[g, my_core],
                core_snd.at[g, 1],
                core_rcv.at[g, 1],
                partner,
            )
        ]

    def start_yz(make, g):
        def body(d, carry):
            make(g, d).start()
            return carry

        lax.fori_loop(1, nyz, body, 0)

    def arrive_yz(make, g):
        def body(d, carry):
            make(g, d).wait_recv()
            return carry

        lax.fori_loop(1, nyz, body, 0)

    def sent_yz(make, g):
        def body(d, carry):
            make(g, d).wait_send()
            return carry

        lax.fori_loop(1, nyz, body, 0)

    def reduce_core(g):
        arrive(core_scatter(g))
        sb[g] = (p32[g, my_core] + r1[g].astype(F32)).astype(BF)
        start(x_scatter(g))

    def reduce_x(g):
        arrive(x_scatter(g))
        total = p32[g, my_core, my_x] + r1[g, my_x].astype(F32)
        for d in range(1, nx):
            total = total + r2[g, d - 1].astype(F32)
        for i in range(nyz):
            s3[g, i] = total[i * piece : (i + 1) * piece]
        start_yz(yz_scatter, g)

    def reduce_yz(g):
        r3[g, me_yz] = s3[g, me_yz]
        arrive_yz(yz_scatter, g)
        total = r3[g, 0]
        for i in range(1, nyz):
            total = total + r3[g, i]
        r4[g, me_yz] = total * scaling
        start_yz(yz_gather, g)

    def gather_yz(g):
        arrive_yz(yz_gather, g)
        for i in range(nyz):
            rowtmp[g, pl.ds(i * piece, piece)] = r4[g, i]
        gfull[g, my_core, my_x] = rowtmp[g].astype(BF)
        start(x_gather(g))

    def gather_x(g):
        arrive(x_gather(g))
        start(core_gather(g))

    def gather_core(g, ref):
        arrive(core_gather(g))
        ref[...] = gfull[g].astype(F32).reshape(basis * chans, chans)

    weight_grad(0, y1, ext_d)
    start(core_scatter(0))

    arrive(halo(2, ext_h))

    def second(b, carry):
        for i in range(blk):
            stencil(ext_h, y2, b * blk + i)
        return carry

    lax.fori_loop(0, nblk, second, 0)
    weight_grad(1, y2, ext_c)
    start(core_scatter(1))
    reduce_core(0)

    def second_mix(b, carry):
        r0 = b * blk
        z = mix(y2, w2_ref, r0).reshape(blk, own, chans)
        out_ref[pl.ds(r0, blk)] = z[:, :cols].astype(BF)
        return carry

    lax.fori_loop(0, nblk, second_mix, 0)
    reduce_x(0)
    reduce_core(1)

    arrive(halo(3, ext_d))
    spread(ext_d, w1_ref)
    reduce_yz(0)
    reduce_x(1)

    def finish(b, carry):
        r0 = b * blk
        gin_ref[pl.ds(r0, blk)] = gathered(r0)[:, :cols].astype(BF)
        return carry

    lax.fori_loop(0, nblk, finish, 0)
    reduce_yz(1)
    gather_yz(0)
    gather_yz(1)
    gather_x(0)
    gather_x(1)
    gather_core(0, g1_ref)
    gather_core(1, g2_ref)

    for field, ext in enumerate((ext_f, ext_c, ext_h, ext_d)):
        for copy in halo(field, ext):
            copy.wait_send()
    for copy in tap_copies():
        copy.wait_send()
    for g in range(2):
        for copy in core_scatter(g) + x_scatter(g) + x_gather(g) + core_gather(g):
            copy.wait_send()
        sent_yz(yz_scatter, g)
        sent_yz(yz_gather, g)


def tap_rows(taps):
    reach = taps.ndim * ((0, 0),)
    half = jnp.pad(taps, reach[:-1] + ((0, WIDE - 2 * HW - 1),))
    return jnp.roll(half, -HW, axis=-1).reshape(taps.shape[0], -1, WIDE)


def local(sizes, features, cotangent, basis, support, weight_one, weight_two):
    nx, nyl, nz, nyh = sizes
    rows, cols, chans = features.shape
    count = weight_one.shape[0]
    nlat, nlon = nx * nyl * 2, nz * nyh
    nyz = nyl * nyh * nz
    scaling = 1.0 / math.sqrt(rows * nlat * cols * nlon)
    own = -(-cols // 16) * 16
    chunk = count * chans // (2 * nx)
    piece = chunk // nyz

    lat = lax.axis_index("lat")
    offset = jnp.abs(jnp.arange(2 * HW + 1, dtype=jnp.int32) - HW)
    inside = offset[None, :] <= support[:, None]
    filtered = jnp.where(inside[:, None, None, :], basis, jnp.zeros_like(basis)).astype(F32)
    row = lax.broadcasted_iota(jnp.int32, (rows, 1, 3, 1), 0) + lat * rows
    side = lax.broadcasted_iota(jnp.int32, (rows, 1, 3, 1), 2) - 1
    exists = (row + side >= 0) & (row + side < rows * nlat)
    fwd_taps = tap_rows(jnp.where(exists, filtered, 0.0))
    back_taps = tap_rows(filtered[..., ::-1])

    vmem = pl.BlockSpec(memory_space=pltpu.VMEM)
    dma = pltpu.SemaphoreType.DMA
    ext = pltpu.VMEM((rows + 2, WIDE, chans), BF)
    out = pl.pallas_call(
        functools.partial(
            kernel, (nx, nyl, nz, nyh, rows, cols, chans, count, scaling)
        ),
        out_shape=(
            jax.ShapeDtypeStruct(features.shape, BF),
            jax.ShapeDtypeStruct(features.shape, BF),
            jax.ShapeDtypeStruct((count * chans, chans), F32),
            jax.ShapeDtypeStruct((count * chans, chans), F32),
        ),
        in_specs=[vmem] * 6,
        out_specs=(vmem,) * 4,
        scratch_shapes=[
            ext,
            ext,
            ext,
            ext,
            pltpu.VMEM((4, rows, HW, chans), BF),
            pltpu.VMEM((rows + 2, count * 3, WIDE), F32),
            pltpu.VMEM((rows, count * own, 3 * WIDE), BF),
            pltpu.VMEM((rows + 2, 3 * own, count * WIDE), BF),
            pltpu.VMEM((rows, own, count * chans), BF),
            pltpu.VMEM((rows, own, count * chans), BF),
            pltpu.VMEM((rows, own, chans), F32),
            pltpu.VMEM((rows + 2, count, WIDE, chans), BF),
            pltpu.VMEM((rows + 2, 3, own, chans), F32),
            pltpu.VMEM((2, 2, nx, chunk, chans), F32),
            pltpu.VMEM((2, nx, chunk, chans), BF),
            pltpu.VMEM((2, nx, chunk, chans), BF),
            pltpu.VMEM((2, nx, chunk, chans), BF),
            pltpu.VMEM((2, nx - 1, chunk, chans), BF),
            pltpu.VMEM((2, nyz, piece, chans), F32),
            pltpu.VMEM((2, nyz, piece, chans), F32),
            pltpu.VMEM((2, nyz, piece, chans), F32),
            pltpu.VMEM((2, chunk, chans), F32),
            pltpu.VMEM((2, 2, nx, chunk, chans), BF),
            dma((4, 8)),
            dma((4, 8)),
            dma((2,)),
            dma((2,)),
            dma((2, 2)),
            dma((2, 2)),
            dma((2, 2, nx)),
            dma((2, 2, nx)),
            dma((2, 2, nyz)),
            dma((2, 2, nyz)),
        ],
        compiler_params=pltpu.CompilerParams(
            collective_id=0, has_side_effects=True, vmem_limit_bytes=60 * 1024 * 1024
        ),
    )(features, cotangent, fwd_taps, back_taps, weight_one, weight_two)
    shape = weight_one.shape
    return out[0], out[1], out[2].reshape(shape), out[3].reshape(shape)


def solution(mesh):
    nlat, nlon = mesh.shape["lat"], mesh.shape["lon"]
    nyl = 2 if nlat >= 16 else 1
    sizes = (nlat // (2 * nyl), nyl, nlon // 2, 2)
    placed = (
        P("lat", "lon", None),
        P("lat", "lon", None),
        P("lat", None, None, None),
        P("lat"),
        P(),
        P(),
    )
    return jax.shard_map(
        functools.partial(local, sizes),
        mesh=mesh,
        in_specs=placed,
        out_specs=(P("lat", "lon", None), P("lat", "lon", None), P(), P()),
        check_vma=False,
    )
```

time: 381 us -> 97.8 us (0.26)
  waiting for transfers between devices: 256 us -> 0 us
  Pallas kernels: 0 us -> 84.7 us
  starting transfers between devices: 44.6 us -> 0 us
  matrix products: 24.4 us -> 0 us
  local copies, waits for them, and re-layouts: 32.9 us -> 10.7 us
  between operations: 14.5 us -> 0.72 us
  other arithmetic: 6.64 us -> 1.28 us
    psum x1 -> x0, waiting for transfers between devices: 237 us -> none  [local(): grad_one, grad_two = lax.psum((grad_one, grad_two), ('lat', 'lon'))]
    pallas_call x0 -> x1, Pallas kernels: none -> 84.7 us  [local(): pl.pallas_call(functools.partial(kernel, (nx, nyl, nz, nyh, rows, cols, c...]
    ppermute x16 -> x0, starting transfers between devices: 44.5 us -> none  [the longest x8 25.5 us: padded(): lax.ppermute(head, axis, [((i + 1) % count, i) for i in range(ends)])]
    dot_general x12 -> x0, matrix products: 24.4 us -> none  [the longest x2 6.22 us: spread(): jnp.einsum('rkaqp,rpkc->arqc', band_back, grad_wide, preferred_element_ty...]
    ppermute x16 -> x0, waiting for transfers between devices: 18.5 us -> none  [the longest x8 11.6 us: padded(): lax.ppermute(head, axis, [((i + 1) % count, i) for i in range(ends)])]
    reshape x6 -> x2, local copies, waits for them, and re-layouts: 12.4 us -> 1.37 us  [tap_rows(): return jnp.roll(half, -HW, axis=-1).reshape(taps.shape[0], -1, WIDE)]
    unnamed x44 -> x20, local copies, waits for them, and re-layouts: 13.4 us -> 8.94 us
  transfers between devices with their start and end apart: 17 -> 0, of which waited for: 7 -> 0; matrix products, arithmetic and copies ran while one was open for 13% -> 0% of each run, Pallas kernels for 0% -> 0%
where the time goes in v1:
time: 97.8 us; the launch traced here: 97.5 us
  Pallas kernels  84.7 us (87%)
  local copies, waits for them, and re-layouts  10.7 us (11%)
  other arithmetic  1.28 us (1%)
    pallas_call x1, Pallas kernels, local(): pl.pallas_call(functools.partial(kernel, (nx, nyl, nz, nyh, rows, cols, c...  84.7 us
    unnamed x20, local copies, waits for them, and re-layouts  8.94 us

profile of v1, /device:TPU:1, one launch (start us, length us, event | category | flops | bytes accessed | tf_op | source)
XLA Modules:
  0.0 97.5 jit_solution(18263954425617771740)
XLA Ops:
  0.7 0.1 fusion
  0.7 0.6 copy-done.6
  1.4 0.1 broadcast_compare_fusion
  1.5 0.9 broadcast_select_fusion
  2.4 0.1 rev.3
  2.5 0.0 copy-start.3
  2.5 0.1 slice.25
  2.6 0.1 slice.23
  2.7 0.1 pad_slice_fusion
  2.8 0.1 pad_maximum_fusion.1
  2.9 0.7 copy.19.tb_ref
  3.5 0.1 pad_slice_fusion.1
  3.6 0.1 pad_maximum_fusion
  3.7 0.7 copy.18.tf_ref
  4.4 1.1 %copy.16.f_ref = bf16[16,90,256]{2,1,0:T(8,128)(2,1)} copy(bf16[16,90,256]{2,0,1:T(8,128)(2,1)S(1)} %copy-done.3) | data formatting | bytes 1474560 | tf_op args[0]
  5.5 0.0 copy-done.4
  5.5 1.1 %copy.17.c_ref = bf16[16,90,256]{2,1,0:T(8,128)(2,1)} copy(bf16[16,90,256]{2,0,1:T(8,128)(2,1)S(1)} %copy-done.4) | data formatting | bytes 1474560 | tf_op args[1]
  6.6 84.7 %shard_map.93 = (bf16[16,90,256]{2,1,0:T(8,128)(2,1)}, bf16[16,90,256]{2,1,0:T(8,128)(2,1)}, f32[768,256]{1,0:T(8,128)}, f32[768,256]{1,0:T(8,128)}) custom-call(bf16[16,90,256]{2,1,0:T(8,128)(2,1)} %copy.16.f_ref, bf16[16,90,256]{2,1,0:T(8,128)(2,1)} %copy.17.c_ref, f32[16,9,128]{2,1,0:T(8,128)} %copy.18.tf_ref, f32[16,9,128]{2,1,0:T(8,128)} %copy.19.tb_ref, ...), custom_call_target="tpu_custom_call" | custom-call | tf_op jit(solution)/shard_map/pallas_call | solution.py:526
  91.4 2.5 %copy.20 = bf16[16,90,256]{2,0,1:T(8,128)(2,1)} copy(bf16[16,90,256]{2,1,0:T(8,128)(2,1)} %get-tuple-element.16) | data formatting | bytes 1474560
  93.9 1.3 %copy.21 = bf16[16,90,256]{2,0,1:T(8,128)(2,1)} copy(bf16[16,90,256]{2,1,0:T(8,128)(2,1)S(1)} %copy-done.2) | data formatting | bytes 1474560
  95.2 0.0 copy-done.1
  95.2 0.9 copy.24
  96.0 0.5 copy-done
  96.6 0.9 copy.25
  (13 shorter events, 0.0 us)
Async XLA Ops:
  0.7 0.7 copy-start.6
  1.5 0.9 copy-start.5
  2.5 1.9 %copy-start.3 = (bf16[16,90,256]{2,0,1:T(8,128)(2,1)S(1)}, bf16[16,90,256]{2,0,1:T(8,128)(2,1)}, u32[]{:S(2)}) copy-start(bf16[16,90,256]{2,0,1:T(8,128)(2,1)} %param.6) | copy-start | bytes 2211844
  4.4 1.1 %copy-start.4 = (bf16[16,90,256]{2,0,1:T(8,128)(2,1)S(1)}, bf16[16,90,256]{2,0,1:T(8,128)(2,1)}, u32[]{:S(2)}) copy-start(bf16[16,90,256]{2,0,1:T(8,128)(2,1)} %param.7) | copy-start | bytes 2211844
  91.4 2.5 %copy-start.2 = (bf16[16,90,256]{2,1,0:T(8,128)(2,1)S(1)}, bf16[16,90,256]{2,1,0:T(8,128)(2,1)}, u32[]{:S(2)}) copy-start(bf16[16,90,256]{2,1,0:T(8,128)(2,1)} %get-tuple-element.17) | copy-start | bytes 2211844
  93.9 1.3 %copy-start.1 = (f32[768,256]{1,0:T(8,128)S(1)}, f32[768,256]{1,0:T(8,128)}, u32[]{:S(2)}) copy-start(f32[768,256]{1,0:T(8,128)} %get-tuple-element.10) | copy-start | bytes 2359300
  95.2 1.4 %copy-start = (f32[768,256]{1,0:T(8,128)S(1)}, f32[768,256]{1,0:T(8,128)}, u32[]{:S(2)}) copy-start(f32[768,256]{1,0:T(8,128)} %get-tuple-element.11) | copy-start | bytes 2359300

commit v2 on v0

v2 whole, which is shorter than its diff:
```python
import functools
import math

import jax
import jax.numpy as jnp
from jax import lax
from jax.experimental import pallas as pl
from jax.experimental.pallas import tpu as pltpu
from jax.sharding import PartitionSpec as P

HW = 16
SPAN = 2 * HW + 1
WIDE = 128
MESH = pl.DeviceIdType.MESH
BF = jnp.bfloat16
F32 = jnp.float32
NN = (((1,), (0,)), ((), ()))
NT = (((1,), (1,)), ((), ()))
TN = (((0,), (0,)), ((), ()))


def dot(a, b, dims=NN):
    return lax.dot_general(a, b, dims, preferred_element_type=F32)


def iota(shape, dim):
    return lax.broadcasted_iota(jnp.int32, shape, dim)


def kernel(
    dims,
    f_ref,
    c_ref,
    basis_ref,
    support_ref,
    w1_ref,
    w2_ref,
    out_ref,
    gin_ref,
    grad_ref,
    raw_f,
    raw_c,
    w1,
    w2,
    w1t,
    w2t,
    perm,
    ext_f,
    ext_c,
    ext_h,
    ext_d,
    tails,
    loose,
    taps,
    edge_out,
    edge_in,
    band,
    back,
    y1,
    v2,
    tmp,
    dsig,
    natural,
    turned,
    p32,
    gb,
    r1,
    sb,
    r2,
    ty,
    sy,
    ry,
    s3,
    r3,
    r4,
    rowtmp,
    gfull,
    in_sem,
    out_sem,
    halo_snd,
    halo_rcv,
    tap_snd,
    tap_rcv,
    core_snd,
    core_rcv,
    x_snd,
    x_rcv,
    y_snd,
    y_rcv,
    z_snd,
    z_rcv,
):
    nx, nyl, nz, nyh, rows, cols, chans, basis, scaling = dims
    own = -(-cols // 16) * 16
    right = own
    left = WIDE - HW
    nlat, nlon = nx * nyl * 2, nz * nyh
    ny = nyl * nyh
    blk = 4
    nblk = rows // blk
    wide_chans = basis * chans

    inputs = [
        pltpu.make_async_copy(src, dst, in_sem.at[i])
        for i, (src, dst) in enumerate(
            [
                (f_ref, raw_f.at[pl.ds(0, cols)]),
                (c_ref, raw_c.at[pl.ds(0, cols)]),
                (w1_ref, w1),
                (w2_ref, w2),
            ]
        )
    ]
    for copy in inputs:
        copy.start()

    lat = lax.axis_index("lat")
    lon = lax.axis_index("lon")

    def wrap(value, count):
        return jnp.where(value >= count, value - count, value)

    my_x = lat // (nyl * 2)
    in_x = lat - my_x * (nyl * 2)
    my_yl = in_x // 2
    my_core = in_x - my_yl * 2
    my_z = lon // nyh
    my_y = (lon - my_z * nyh) * nyl + my_yl
    north, south = wrap(lat + nlat - 1, nlat), wrap(lat + 1, nlat)
    west, east = wrap(lon + nlon - 1, nlon), wrap(lon + 1, nlon)

    partner = (lat + 1 - 2 * my_core, lon)
    around = [
        (lat, east),
        (lat, west),
        (south, lon),
        (north, lon),
        (south, east),
        (north, east),
        (south, west),
        (north, west),
    ]
    x_peers = [wrap(my_x + d, nx) for d in range(nx)]
    x_devices = [(x * (nyl * 2) + in_x, lon) for x in x_peers]
    x_from = [wrap(my_x + nx - d, nx) for d in range(nx)]
    y_peers = [wrap(my_y + d, ny) for d in range(ny)]
    z_peers = [wrap(my_z + d, nz) for d in range(nz)]
    my_yh = lon - my_z * nyh
    y_devices = []
    for y in y_peers:
        yh = y // nyl
        y_devices.append((my_x * (nyl * 2) + (y - yh * nyl) * 2 + my_core, my_z * nyh + yh))
    z_devices = [(lat, z * nyh + my_yh) for z in z_peers]

    barrier = pltpu.get_barrier_semaphore()

    def greet(device):
        pl.semaphore_signal(barrier, inc=1, device_id=device, device_id_type=MESH)

    for device in around:
        greet(device)
    others = z_devices[1:] + x_devices[1:] + y_devices[1:] + [partner]
    for device in others:
        greet(device)

    side = HW * HW
    i0, i1 = iota((side, side), 0), iota((side, side), 1)
    perm[...] = jnp.where(i1 == (i0 & 15) * HW + (i0 >> 4), 1.0, 0.0).astype(BF)

    def turn(block):
        return dot(perm[...], block.reshape(side, chans)).astype(BF).reshape(HW, HW, chans)

    def stage(field, raw, ext):
        raw[pl.ds(cols, own - cols)] = jnp.zeros((own - cols, rows, chans), BF)
        tails[field] = turn(raw[pl.ds(cols - HW, HW)])
        for b in range(own // HW):
            ext[pl.ds(1, rows), pl.ds(b * HW, HW)] = turn(raw[pl.ds(b * HW, HW)])

    def remote(src, dst, snd, rcv, device):
        return pltpu.make_async_remote_copy(
            src_ref=src,
            dst_ref=dst,
            send_sem=snd,
            recv_sem=rcv,
            device_id=device,
            device_id_type=MESH,
        )

    def halo(field, ext, parts=(0, 1)):
        tail = tails.at[field]
        top = rows // 2 + 1
        upper, lower = pl.ds(1, top), pl.ds(1 + top, rows - top)
        moves = [
            [
                (tail.at[pl.ds(0, top)], ext.at[upper, pl.ds(left, HW)], 0),
                (ext.at[upper, pl.ds(0, HW)], ext.at[upper, pl.ds(right, HW)], 1),
                (ext.at[rows, pl.ds(0, own)], ext.at[0, pl.ds(0, own)], 2),
                (tail.at[rows - 1], ext.at[0, pl.ds(left, HW)], 4),
                (ext.at[rows, pl.ds(0, HW)], ext.at[0, pl.ds(right, HW)], 6),
            ],
            [
                (tail.at[pl.ds(top, rows - top)], ext.at[lower, pl.ds(left, HW)], 0),
                (ext.at[lower, pl.ds(0, HW)], ext.at[lower, pl.ds(right, HW)], 1),
                (ext.at[1, pl.ds(0, own)], ext.at[rows + 1, pl.ds(0, own)], 3),
                (tail.at[0], ext.at[rows + 1, pl.ds(left, HW)], 5),
                (ext.at[1, pl.ds(0, HW)], ext.at[rows + 1, pl.ds(right, HW)], 7),
            ],
        ]
        return [
            remote(src, dst, halo_snd.at[field, part, i], halo_rcv.at[field, part, i], around[to])
            for part in parts
            for i, (src, dst, to) in enumerate(moves[part])
        ]

    def tap_copies():
        return [
            remote(edge_out.at[i], edge_in.at[i], tap_snd.at[i], tap_rcv.at[i], device)
            for i, device in enumerate([(south, lon), (north, lon)])
        ]

    def start(copies):
        for copy in copies:
            copy.start()

    def arrive(copies):
        for copy in copies:
            copy.wait_recv()

    def sent(copies):
        for copy in copies:
            copy.wait_send()

    inputs[0].wait()
    stage(0, raw_f, ext_f)
    pl.semaphore_wait(barrier, len(around) + len(others))
    start(halo(0, ext_f))

    loose[...] = jnp.zeros(loose.shape, F32)
    row = iota((rows, WIDE), 0)
    lane = iota((rows, WIDE), 1)
    reach = jnp.zeros((rows, WIDE), jnp.int32)
    for r in range(rows):
        reach = jnp.where(row == r, support_ref[r], reach)
    inside = jnp.abs(lane - HW) <= reach
    for k in range(basis):
        for a in range(3):
            loose[k * 3 + a, :, pl.ds(0, SPAN)] = basis_ref[k, a].astype(F32)
    b0, b1 = iota((WIDE, 2 * WIDE), 0), iota((WIDE, 2 * WIDE), 1)
    place = (b1 == ((b0 - HW) & (WIDE - 1))) | (b1 == ((HW - b0) & (WIDE - 1)) + WIDE)
    place = jnp.where(place, 1.0, 0.0).astype(BF)
    for k in range(basis):
        for a in range(3):
            ka = k * 3 + a
            masked = jnp.where(inside, loose[ka], 0.0).astype(BF)
            placed = dot(masked, place)
            edge_out[0, pl.ds(ka, 1)] = placed[rows - 1 : rows, WIDE:]
            edge_out[1, pl.ds(ka, 1)] = placed[:1, WIDE:]
            forward = placed[:, :WIDE]
            if a == 0:
                forward = jnp.where((row == 0) & (lat == 0), 0.0, forward)
            elif a == 2:
                forward = jnp.where((row == rows - 1) & (lat == nlat - 1), 0.0, forward)
            for r in range(rows):
                taps[r, pl.ds(ka, 1), pl.ds(0, WIDE)] = forward[r : r + 1]
                taps[r, pl.ds(ka, 1), pl.ds(WIDE, WIDE)] = placed[r : r + 1, WIDE:]
    start(tap_copies())

    low = own - 24
    lane24 = iota((24, WIDE), 1)
    valid = iota((24, WIDE), 0) + low < cols
    plain = valid & ((lane24 < cols) | (lane24 >= left))
    moved = valid & (lane24 >= right) & (lane24 < left)
    gap = own - cols

    def toeplitz(tap):
        wide = jnp.broadcast_to(tap, (own, WIDE))
        t = pltpu.roll(wide, 0, 1, stride=1, stride_axis=0)
        t6 = pltpu.roll(wide[:24], low + gap, 1, stride=1, stride_axis=0)
        bottom = jnp.where(moved, t6, jnp.where(plain, t[low:], 0.0))
        return jnp.concatenate([t[:low], bottom], axis=0).astype(BF)

    def build_fwd(r, carry):
        for k in range(basis):
            for a in range(3):
                tap = taps[r, pl.ds(k * 3 + a, 1), pl.ds(0, WIDE)]
                band[r, pl.ds(k * own, own), pl.ds(a * WIDE, WIDE)] = toeplitz(tap)
        return carry

    def build_back(r, carry):
        for k in range(basis):
            for a in range(3):
                tap = taps[r, pl.ds(k * 3 + a, 1), pl.ds(WIDE, WIDE)]
                t = 2 - a
                back[r + a, pl.ds(k * own, own), pl.ds(t * WIDE, WIDE)] = toeplitz(tap)
        return carry

    lax.fori_loop(0, rows, build_fwd, 0)

    inputs[1].wait()
    stage(1, raw_c, ext_c)
    inputs[2].wait()
    inputs[3].wait()
    eye = jnp.where(iota((chans, chans), 0) == iota((chans, chans), 1), 1.0, 0.0).astype(BF)
    for k in range(basis):
        w1t[k] = dot(eye, w1[k], NT).astype(BF)
        w2t[k] = dot(eye, w2[k], NT).astype(BF)
    lax.fori_loop(0, rows, build_back, 0)

    def stencil(ext, matrix, at, y, r):
        x = ext[pl.ds(r, 3)].reshape(3 * WIDE, chans)
        t = dot(matrix[r + at], x).astype(BF)
        for k in range(basis):
            y[r, :, pl.ds(k * chans, chans)] = t[k * own : (k + 1) * own]

    def convolve(ext, matrix, at, y, w, r0):
        for i in range(blk):
            stencil(ext, matrix, at, y, r0 + i)
        flat = y[pl.ds(r0, blk)].reshape(blk * own, wide_chans)
        return dot(flat, w[...].reshape(wide_chans, chans))

    def put(field, ext, r0, value):
        value = value.reshape(blk, own, chans)
        ext[pl.ds(r0 + 1, blk), pl.ds(0, own)] = value.astype(BF)
        for i in range(blk):
            tails[field, r0 + i] = value[i, cols - HW : cols].astype(BF)

    def first(b, carry):
        r0 = b * blk
        z = convolve(ext_f, band, 0, y1, w1, r0)
        sigma = jax.nn.sigmoid(z)
        dsig[pl.ds(r0, blk)] = (sigma * (1.0 + z * (1.0 - sigma))).reshape(blk, own, chans)
        put(2, ext_h, r0, z * sigma)
        return carry

    def first_back(b, carry):
        r0 = b * blk
        g = convolve(ext_c, back, 1, v2, w2t, r0)
        put(3, ext_d, r0, g * dsig[pl.ds(r0, blk)].reshape(blk * own, chans))
        return carry

    def second(b, carry):
        r0 = b * blk
        z = convolve(ext_h, band, 0, tmp, w2, r0)
        natural[0, pl.ds(r0, blk)] = z.astype(BF).reshape(blk, own, chans)
        return carry

    def second_back(b, carry):
        r0 = b * blk
        z = convolve(ext_d, back, 1, tmp, w1t, r0)
        natural[1, pl.ds(r0, blk)] = z.astype(BF).reshape(blk, own, chans)
        return carry

    def outgoing(i, ref):
        return pltpu.make_async_copy(turned.at[i, pl.ds(0, cols)], ref, out_sem.at[i])

    def emit(i, ref):
        for b in range(own // HW):
            turned[i, pl.ds(b * HW, HW)] = turn(natural[i, :, pl.ds(b * HW, HW)])
        outgoing(i, ref).start()

    chunk = wide_chans // nx
    half = chunk // 2
    slab = chunk // ny
    piece = slab // nz
    far_first = sorted(range(1, nx), key=lambda d: -min(d, nx - d))
    near_first = far_first[::-1]

    def core_scatter(d):
        x = x_peers[d]
        return remote(gb.at[x], r1.at[x], core_snd.at[0, d], core_rcv.at[0, d], partner)

    def x_scatter(d):
        src, dst = sb.at[x_peers[d]], r2.at[d - 1]
        return remote(src, dst, x_snd.at[0, d], x_rcv.at[0, d], x_devices[d])

    def y_scatter(d):
        src, dst = sy.at[y_peers[d]], ry.at[d - 1]
        return remote(src, dst, y_snd.at[0, d], y_rcv.at[0, d], y_devices[d])

    def z_scatter(d):
        src, dst = s3.at[z_peers[d]], r3.at[d - 1]
        return remote(src, dst, z_snd.at[0, d], z_rcv.at[0, d], z_devices[d])

    def z_gather(d):
        mine = r4.at[my_z]
        return remote(mine, mine, z_snd.at[1, d], z_rcv.at[1, d], z_devices[d])

    def y_gather(d):
        mine = gfull.at[my_core, my_x, my_y]
        return remote(mine, mine, y_snd.at[1, d], y_rcv.at[1, d], y_devices[d])

    def x_gather(d):
        mine = gfull.at[my_core, my_x]
        return remote(mine, mine, x_snd.at[1, d], x_rcv.at[1, d], x_devices[d])

    def core_gather(d):
        mine = gfull.at[my_core, x_from[d]]
        return remote(mine, mine, core_snd.at[1, d], core_rcv.at[1, d], partner)

    def every(make, count):
        return [make(d) for d in range(1, count)]

    def keep_grad(g, value, first):
        for core in range(2):
            for x in range(nx):
                at = (core * nx + x) * half
                to = (core, x, pl.ds(g * half, half))
                share = value[at : at + half]
                p32[to] = share if first else p32[to] + share

    def reduce_core():
        for d in far_first:
            x = x_peers[d]
            core_scatter(d).wait_recv()
            sb[x] = (p32[my_core, x] + r1[x].astype(F32)).astype(BF)
            x_scatter(d).start()
        core_scatter(0).wait_recv()

    def reduce_x():
        arrive(every(x_scatter, nx))
        total = p32[my_core, my_x] + r1[my_x].astype(F32)
        for d in range(1, nx):
            total = total + r2[d - 1].astype(F32)
        ty[...] = total.reshape(ny, slab, chans)
        sy[...] = total.astype(BF).reshape(ny, slab, chans)
        start(every(y_scatter, ny))

    def reduce_y():
        arrive(every(y_scatter, ny))
        total = ty[my_y]
        for d in range(1, ny):
            total = total + ry[d - 1].astype(F32)
        for i in range(nz):
            s3[i] = total[i * piece : (i + 1) * piece]
        start(every(z_scatter, nz))

    def reduce_z():
        arrive(every(z_scatter, nz))
        r4[my_z] = (s3[my_z] + jnp.sum(r3[...], axis=0)) * scaling
        start(every(z_gather, nz))

    def gather_z():
        arrive(every(z_gather, nz))
        for i in range(nz):
            rowtmp[pl.ds(i * piece, piece)] = r4[i]
        gfull[my_core, my_x, my_y] = rowtmp[...].astype(BF)
        start(every(y_gather, ny))

    def gather_y():
        arrive(every(y_gather, ny))
        start([x_gather(d) for d in far_first])
        core_gather(0).start()

    def gather_x():
        for d in near_first:
            x_gather(d).wait_recv()
            core_gather(d).start()
        for d in range(nx):
            core_gather(d).wait_recv()

    def mine(ext, r0, count):
        return ext[pl.ds(r0 + 1, count), pl.ds(0, own)].reshape(count * own, chans)

    def weight_grads(r0, count, first):
        flat = v2[pl.ds(r0, count)].reshape(count * own, wide_chans)
        grad = dot(mine(ext_h, r0, count), flat, TN)
        parts = [grad[:, k * chans : (k + 1) * chans] for k in range(basis)]
        keep_grad(1, jnp.concatenate(parts, 0), first)
        flat = y1[pl.ds(r0, count)].reshape(count * own, wide_chans)
        keep_grad(0, dot(flat, mine(ext_d, r0, count), TN), first)

    def halves(field, ext, body, between=None):
        for part in range(2):
            arrive(halo(field, ext, (part,)))
            lax.fori_loop(part * nblk // 2, (part + 1) * nblk // 2, body, 0)
            if between is not None:
                between(part)

    sent(halo(0, ext_f))
    start(halo(1, ext_c))
    halves(0, ext_f, first)
    sent(halo(1, ext_c))
    start(halo(2, ext_h))

    arrive(tap_copies())
    for k in range(basis):
        tap = jnp.where(lat > 0, edge_in[0, pl.ds(k * 3 + 2, 1)], 0.0)
        back[1, pl.ds(k * own, own), pl.ds(0, WIDE)] = toeplitz(tap)
        tap = jnp.where(lat < nlat - 1, edge_in[1, pl.ds(k * 3, 1)], 0.0)
        back[rows, pl.ds(k * own, own), pl.ds(2 * WIDE, WIDE)] = toeplitz(tap)
    halves(
        1,
        ext_c,
        first_back,
        lambda part: weight_grads(part * (rows // 2), rows // 2, part == 0),
    )
    gb[...] = p32[1 - my_core].astype(BF)
    start([core_scatter(d) for d in far_first + [0]])
    reduce_core()
    sent(halo(2, ext_h))
    start(halo(3, ext_d))

    halves(2, ext_h, second)
    emit(0, out_ref)
    reduce_x()
    reduce_y()
    halves(3, ext_d, second_back, lambda part: reduce_z() if part == 0 else None)
    gather_z()
    emit(1, gin_ref)
    gather_y()
    gather_x()
    last = pltpu.make_async_copy(gfull, grad_ref, out_sem.at[2])
    last.start()

    sent(halo(3, ext_d) + tap_copies())
    sent([make(d) for make in (core_scatter, core_gather) for d in range(nx)])
    sent(every(x_scatter, nx) + every(x_gather, nx))
    sent(every(y_scatter, ny) + every(y_gather, ny))
    sent(every(z_scatter, nz) + every(z_gather, nz))
    outgoing(0, out_ref).wait()
    outgoing(1, gin_ref).wait()
    last.wait()


def deliver(nx, half, out_in, gin_in, grad_in, out_ref, gin_ref, g1_ref, g2_ref, *scratch):
    out, gin, grad, g1, g2, in_sems, out_sems = scratch
    cells = out.shape[0]
    cut = cells // 2

    def put(i, src, dst, sems):
        return pltpu.make_async_copy(src, dst, sems.at[i])

    steps = [(4, grad_in, grad)]
    for i, (src, dst) in enumerate([(out_in, out), (gin_in, gin)]):
        steps += [(2 * i + j, src.at[at], dst.at[at]) for j, at in enumerate(parts_of(cells, cut))]
    arriving = [put(i, src, dst, in_sems) for i, src, dst in steps]
    for copy in arriving:
        copy.start()
    arriving[0].wait()
    for core in range(2):
        for x in range(nx):
            at = pl.ds((core * nx + x) * half, half)
            flat = grad[core, x].reshape(2 * half, grad.shape[-1]).astype(F32)
            g1[at] = flat[:half]
            g2[at] = flat[half:]
    leaving = [put(4, g1, g1_ref, out_sems), put(5, g2, g2_ref, out_sems)]
    for copy in leaving:
        copy.start()
    for i, (src, dst) in enumerate([(out, out_ref), (gin, gin_ref)]):
        for j, at in enumerate(parts_of(cells, cut)):
            arriving[1 + 2 * i + j].wait()
            copy = put(2 * i + j, src.at[at], dst.at[at], out_sems)
            copy.start()
            leaving.append(copy)
    for copy in leaving:
        copy.wait()


def parts_of(count, cut):
    return pl.ds(0, cut), pl.ds(cut, count - cut)


def local(sizes, features, cotangent, basis, support, weight_one, weight_two):
    nx, nyl, nz, nyh = sizes
    rows, cols, chans = features.shape
    count = weight_one.shape[0]
    nlat, nlon = nx * nyl * 2, nz * nyh
    ny = nyl * nyh
    scaling = 1.0 / math.sqrt(rows * nlat * cols * nlon)
    own = -(-cols // 16) * 16
    chunk = count * chans // nx
    slab = chunk // ny
    piece = slab // nz

    vmem = pl.BlockSpec(memory_space=pltpu.VMEM)
    smem = pl.BlockSpec(memory_space=pltpu.SMEM)
    hbm = pl.BlockSpec(memory_space=pl.ANY)
    dma = pltpu.SemaphoreType.DMA
    ext = pltpu.VMEM((rows + 2, WIDE, chans), BF)
    field = jax.ShapeDtypeStruct((cols, rows, chans), BF)
    out, gin, grads = pl.pallas_call(
        functools.partial(kernel, (nx, nyl, nz, nyh, rows, cols, chans, count, scaling)),
        out_shape=(field, field, jax.ShapeDtypeStruct((2, nx, ny, slab, chans), BF)),
        in_specs=[hbm, hbm, vmem, smem, hbm, hbm],
        out_specs=(hbm,) * 3,
        scratch_shapes=[
            pltpu.VMEM((own, rows, chans), BF),
            pltpu.VMEM((own, rows, chans), BF),
            pltpu.VMEM((count, chans, chans), BF),
            pltpu.VMEM((count, chans, chans), BF),
            pltpu.VMEM((count, chans, chans), BF),
            pltpu.VMEM((count, chans, chans), BF),
            pltpu.VMEM((HW * HW, HW * HW), BF),
            ext,
            ext,
            ext,
            ext,
            pltpu.VMEM((4, rows, HW, chans), BF),
            pltpu.VMEM((count * 3, rows, WIDE), F32),
            pltpu.VMEM((rows, count * 3, 2 * WIDE), F32),
            pltpu.VMEM((2, count * 3, WIDE), F32),
            pltpu.VMEM((2, count * 3, WIDE), F32),
            pltpu.VMEM((rows, count * own, 3 * WIDE), BF),
            pltpu.VMEM((rows + 2, count * own, 3 * WIDE), BF),
            pltpu.VMEM((rows, own, count * chans), BF),
            pltpu.VMEM((rows, own, count * chans), BF),
            pltpu.VMEM((rows, own, count * chans), BF),
            pltpu.VMEM((rows, own, chans), F32),
            pltpu.VMEM((2, rows, own, chans), BF),
            pltpu.VMEM((2, own, rows, chans), BF),
            pltpu.VMEM((2, nx, chunk, chans), F32),
            pltpu.VMEM((nx, chunk, chans), BF),
            pltpu.VMEM((nx, chunk, chans), BF),
            pltpu.VMEM((nx, chunk, chans), BF),
            pltpu.VMEM((nx - 1, chunk, chans), BF),
            pltpu.VMEM((ny, slab, chans), F32),
            pltpu.VMEM((ny, slab, chans), BF),
            pltpu.VMEM((ny - 1, slab, chans), BF),
            pltpu.VMEM((nz, piece, chans), F32),
            pltpu.VMEM((nz - 1, piece, chans), F32),
            pltpu.VMEM((nz, piece, chans), F32),
            pltpu.VMEM((slab, chans), F32),
            pltpu.VMEM((2, nx, ny, slab, chans), BF),
            dma((4,)),
            dma((3,)),
            dma((4, 2, 5)),
            dma((4, 2, 5)),
            dma((2,)),
            dma((2,)),
            dma((2, nx)),
            dma((2, nx)),
            dma((2, nx)),
            dma((2, nx)),
            dma((2, ny)),
            dma((2, ny)),
            dma((2, nz)),
            dma((2, nz)),
        ],
        compiler_params=pltpu.CompilerParams(
            collective_id=0, has_side_effects=True, vmem_limit_bytes=60 * 1024 * 1024
        ),
    )(
        features.transpose(1, 0, 2),
        cotangent.transpose(1, 0, 2),
        basis.transpose(1, 2, 0, 3),
        support,
        weight_one,
        weight_two,
    )
    weights = jax.ShapeDtypeStruct((count * chans, chans), F32)
    out, gin, g1, g2 = pl.pallas_call(
        functools.partial(deliver, nx, chunk // 2),
        out_shape=(field, field, weights, weights),
        in_specs=[hbm] * 3,
        out_specs=(hbm,) * 4,
        scratch_shapes=[
            pltpu.VMEM(field.shape, BF),
            pltpu.VMEM(field.shape, BF),
            pltpu.VMEM(grads.shape, BF),
            pltpu.VMEM(weights.shape, F32),
            pltpu.VMEM(weights.shape, F32),
            dma((5,)),
            dma((6,)),
        ],
        compiler_params=pltpu.CompilerParams(vmem_limit_bytes=60 * 1024 * 1024),
    )(out, gin, grads)
    shape = weight_one.shape
    return out.transpose(1, 0, 2), gin.transpose(1, 0, 2), g1.reshape(shape), g2.reshape(shape)


def solution(mesh):
    nlat, nlon = mesh.shape["lat"], mesh.shape["lon"]
    nyl = 2 if nlat >= 16 else 1
    sizes = (nlat // (2 * nyl), nyl, nlon // 2, 2)
    placed = (
        P("lat", "lon", None),
        P("lat", "lon", None),
        P("lat", None, None, None),
        P("lat"),
        P(),
        P(),
    )
    return jax.shard_map(
        functools.partial(local, sizes),
        mesh=mesh,
        in_specs=placed,
        out_specs=(P("lat", "lon", None), P("lat", "lon", None), P(), P()),
        check_vma=False,
    )
```

time: 381 us -> 72.4 us (0.19)
  waiting for transfers between devices: 256 us -> 0 us
  Pallas kernels: 0 us -> 71.6 us
  starting transfers between devices: 44.6 us -> 0 us
  local copies, waits for them, and re-layouts: 32.9 us -> 0 us
  matrix products: 24.4 us -> 0 us
  between operations: 14.5 us -> 0.64 us
  other arithmetic: 6.64 us -> 0 us
    psum x1 -> x0, waiting for transfers between devices: 237 us -> none  [local(): grad_one, grad_two = lax.psum((grad_one, grad_two), ('lat', 'lon'))]
    pallas_call x0 -> x2, Pallas kernels: none -> 71.6 us  [the longest x1 68.7 us: local(): pl.pallas_call(functools.partial(kernel, (nx, nyl, nz, nyh, rows, cols, c...]
    ppermute x16 -> x0, starting transfers between devices: 44.5 us -> none  [the longest x8 25.5 us: padded(): lax.ppermute(head, axis, [((i + 1) % count, i) for i in range(ends)])]
    dot_general x12 -> x0, matrix products: 24.4 us -> none  [the longest x2 6.22 us: spread(): jnp.einsum('rkaqp,rpkc->arqc', band_back, grad_wide, preferred_element_ty...]
    ppermute x16 -> x0, waiting for transfers between devices: 18.5 us -> none  [the longest x8 11.6 us: padded(): lax.ppermute(head, axis, [((i + 1) % count, i) for i in range(ends)])]
    unnamed x44 -> x0, local copies, waits for them, and re-layouts: 13.4 us -> none
    reshape x6 -> x0, local copies, waits for them, and re-layouts: 12.4 us -> none  [the longest x4 12 us: back_mix(): flat.astype(jnp.bfloat16)]
  transfers between devices with their start and end apart: 17 -> 0, of which waited for: 7 -> 0; matrix products, arithmetic and copies ran while one was open for 13% -> 0% of each run, Pallas kernels for 0% -> 0%
where the time goes in v2:
time: 72.4 us; the launch traced here: 72.2 us
  Pallas kernels  71.6 us (99%)
    pallas_call x1, Pallas kernels, local(): pl.pallas_call(functools.partial(kernel, (nx, nyl, nz, nyh, rows, cols, c...  68.7 us
    pallas_call x1, Pallas kernels, local(): pl.pallas_call(functools.partial(deliver, nx, chunk // 2), out_shape=(fie...  2.9 us

profile of v2, /device:TPU:1, one launch (start us, length us, event | category | flops | bytes accessed | tf_op | source)
XLA Modules:
  0.0 72.2 jit_solution(15281755633088399595)
XLA Ops:
  0.6 68.7 %shard_map.93 = (bf16[90,16,256]{2,1,0:T(8,128)(2,1)}, bf16[90,16,256]{2,1,0:T(8,128)(2,1)}, bf16[2,4,4,48,256]{4,3,2,1,0:T(8,128)(2,1)}) custom-call(bf16[90,16,256]{2,1,0:T(8,128)(2,1)} %bitcast.7, bf16[90,16,256]{2,1,0:T(8,128)(2,1)} %bitcast.8, bf16[3,3,16,33]{3,2,1,0:T(8,128)(2,1)} %bitcast.9, s32[16]{0:T(128)} %support_ref.1, ...), custom_call_target="tpu_custom_call" | custom-call | tf_op jit(solution)/shard_map/pallas_call | solution.py:581
  69.3 2.9 %shard_map.94 = (bf16[90,16,256]{2,1,0:T(8,128)(2,1)}, bf16[90,16,256]{2,1,0:T(8,128)(2,1)}, f32[768,256]{1,0:T(8,128)}, f32[768,256]{1,0:T(8,128)}) custom-call(bf16[90,16,256]{2,1,0:T(8,128)(2,1)} %get-tuple-element.11.out_in, bf16[90,16,256]{2,1,0:T(8,128)(2,1)} %get-tuple-element.12.gin_in, bf16[2,4,4,48,256]{4,3,2,1,0:T(8,128)(2,1)} %get-tuple-element.13.grad_in), custom_call_target="tpu_custom_call" | custom-call | tf_op jit(solution)/shard_map/pallas_call | solution.py:651

commit v3 on v2

--- a/solution.py
+++ b/solution.py
@@ -67,13 +67,7 @@
     r1,
     sb,
     r2,
-    ty,
-    sy,
-    ry,
-    s3,
-    r3,
-    r4,
-    rowtmp,
+    zall,
     gfull,
     in_sem,
     out_sem,
@@ -83,10 +77,8 @@
     tap_rcv,
     core_snd,
     core_rcv,
-    x_snd,
-    x_rcv,
-    y_snd,
-    y_rcv,
+    xy_snd,
+    xy_rcv,
     z_snd,
     z_rcv,
 ):
@@ -141,15 +133,16 @@
         (north, west),
     ]
     x_peers = [wrap(my_x + d, nx) for d in range(nx)]
-    x_devices = [(x * (nyl * 2) + in_x, lon) for x in x_peers]
     x_from = [wrap(my_x + nx - d, nx) for d in range(nx)]
     y_peers = [wrap(my_y + d, ny) for d in range(ny)]
     z_peers = [wrap(my_z + d, nz) for d in range(nz)]
     my_yh = lon - my_z * nyh
-    y_devices = []
-    for y in y_peers:
+    xy_devices = {}
+    for dy, y in enumerate(y_peers):
         yh = y // nyl
-        y_devices.append((my_x * (nyl * 2) + (y - yh * nyl) * 2 + my_core, my_z * nyh + yh))
+        for dx, x in enumerate(x_peers):
+            to = (x * (nyl * 2) + (y - yh * nyl) * 2 + my_core, my_z * nyh + yh)
+            xy_devices[dx, dy] = to
     z_devices = [(lat, z * nyh + my_yh) for z in z_peers]
 
     barrier = pltpu.get_barrier_semaphore()
@@ -159,7 +152,7 @@
 
     for device in around:
         greet(device)
-    others = z_devices[1:] + x_devices[1:] + y_devices[1:] + [partner]
+    others = z_devices[1:] + list(xy_devices.values())[1:] + [partner]
     for device in others:
         greet(device)
 
@@ -265,19 +258,23 @@
                 taps[r, pl.ds(ka, 1), pl.ds(WIDE, WIDE)] = placed[r : r + 1, WIDE:]
     start(tap_copies())
 
-    low = own - 24
-    lane24 = iota((24, WIDE), 1)
-    valid = iota((24, WIDE), 0) + low < cols
-    plain = valid & ((lane24 < cols) | (lane24 >= left))
-    moved = valid & (lane24 >= right) & (lane24 < left)
+    low_tiles = [own - 2 * HW, own - HW]
+    at = iota((HW, WIDE), 1)
+    plain, moved = [], []
+    for j in low_tiles:
+        valid = iota((HW, WIDE), 0) + j < cols
+        plain.append(valid & ((at < cols) | (at >= left)))
+        moved.append(valid & (at >= right) & (at < left))
     gap = own - cols
 
     def toeplitz(tap):
-        wide = jnp.broadcast_to(tap, (own, WIDE))
-        t = pltpu.roll(wide, 0, 1, stride=1, stride_axis=0)
-        t6 = pltpu.roll(wide[:24], low + gap, 1, stride=1, stride_axis=0)
-        bottom = jnp.where(moved, t6, jnp.where(plain, t[low:], 0.0))
-        return jnp.concatenate([t[:low], bottom], axis=0).astype(BF)
+        wide = jnp.broadcast_to(tap, (HW, WIDE))
+        tile = pltpu.roll(wide, 0, 1, stride=1, stride_axis=0).astype(BF)
+        tiles = [tile] + [pltpu.roll(tile, j, 1) for j in range(HW, own, HW)]
+        for i, j in enumerate(low_tiles):
+            shifted = pltpu.roll(tile, j + gap, 1)
+            tiles[j // HW] = jnp.where(moved[i], shifted, jnp.where(plain[i], tiles[j // HW], 0))
+        return jnp.concatenate(tiles, axis=0)
 
     def build_fwd(r, carry):
         for k in range(basis):
@@ -361,44 +358,33 @@
     chunk = wide_chans // nx
     half = chunk // 2
     slab = chunk // ny
-    piece = slab // nz
-    far_first = sorted(range(1, nx), key=lambda d: -min(d, nx - d))
+    far_first = sorted(range(nx), key=lambda d: -min(d, nx - d))
     near_first = far_first[::-1]
+    far_first_y = sorted(range(ny), key=lambda d: -min(d, ny - d))
 
     def core_scatter(d):
         x = x_peers[d]
         return remote(gb.at[x], r1.at[x], core_snd.at[0, d], core_rcv.at[0, d], partner)
 
-    def x_scatter(d):
-        src, dst = sb.at[x_peers[d]], r2.at[d - 1]
-        return remote(src, dst, x_snd.at[0, d], x_rcv.at[0, d], x_devices[d])
-
-    def y_scatter(d):
-        src, dst = sy.at[y_peers[d]], ry.at[d - 1]
-        return remote(src, dst, y_snd.at[0, d], y_rcv.at[0, d], y_devices[d])
-
-    def z_scatter(d):
-        src, dst = s3.at[z_peers[d]], r3.at[d - 1]
-        return remote(src, dst, z_snd.at[0, d], z_rcv.at[0, d], z_devices[d])
-
-    def z_gather(d):
-        mine = r4.at[my_z]
-        return remote(mine, mine, z_snd.at[1, d], z_rcv.at[1, d], z_devices[d])
-
-    def y_gather(d):
-        mine = gfull.at[my_core, my_x, my_y]
-        return remote(mine, mine, y_snd.at[1, d], y_rcv.at[1, d], y_devices[d])
-
-    def x_gather(d):
-        mine = gfull.at[my_core, my_x]
-        return remote(mine, mine, x_snd.at[1, d], x_rcv.at[1, d], x_devices[d])
+    def xy_scatter(dx, dy):
+        i = dx * ny + dy
+        src = sb.at[x_peers[dx], y_peers[dy]]
+        return remote(src, r2.at[i], xy_snd.at[0, i], xy_rcv.at[0, i], xy_devices[dx, dy])
+
+    def z_spread(d):
+        own_slab = zall.at[my_z]
+        return remote(own_slab, own_slab, z_snd.at[d], z_rcv.at[d], z_devices[d])
+
+    def xy_gather(dx, dy):
+        i = dx * ny + dy
+        own_slab = gfull.at[my_core, my_x, my_y]
+        return remote(own_slab, own_slab, xy_snd.at[1, i], xy_rcv.at[1, i], xy_devices[dx, dy])
 
     def core_gather(d):
-        mine = gfull.at[my_core, x_from[d]]
-        return remote(mine, mine, core_snd.at[1, d], core_rcv.at[1, d], partner)
-
-    def every(make, count):
-        return [make(d) for d in range(1, count)]
+        arrived = gfull.at[my_core, x_from[d]]
+        return remote(arrived, arrived, core_snd.at[1, d], core_rcv.at[1, d], partner)
+
+    xy_order = [(dx, dy) for dx in far_first for dy in far_first_y if dx + dy > 0]
 
     def keep_grad(g, value, first):
         for core in range(2):
@@ -409,54 +395,37 @@
                 p32[to] = share if first else p32[to] + share
 
     def reduce_core():
-        for d in far_first:
-            x = x_peers[d]
-            core_scatter(d).wait_recv()
-            sb[x] = (p32[my_core, x] + r1[x].astype(F32)).astype(BF)
-            x_scatter(d).start()
-        core_scatter(0).wait_recv()
-
-    def reduce_x():
-        arrive(every(x_scatter, nx))
-        total = p32[my_core, my_x] + r1[my_x].astype(F32)
-        for d in range(1, nx):
-            total = total + r2[d - 1].astype(F32)
-        ty[...] = total.reshape(ny, slab, chans)
-        sy[...] = total.astype(BF).reshape(ny, slab, chans)
-        start(every(y_scatter, ny))
-
-    def reduce_y():
-        arrive(every(y_scatter, ny))
-        total = ty[my_y]
-        for d in range(1, ny):
-            total = total + ry[d - 1].astype(F32)
-        for i in range(nz):
-            s3[i] = total[i * piece : (i + 1) * piece]
-        start(every(z_scatter, nz))
+        for dx in far_first:
+            x = x_peers[dx]
+            core_scatter(dx).wait_recv()
+            total = p32[my_core, x].reshape(ny, slab, chans) + r1[x].astype(F32)
+            sb[x] = total.astype(BF)
+            start([xy_scatter(*to) for to in xy_order if to[0] == dx])
+
+    def reduce_xy():
+        total = p32[my_core, my_x, pl.ds(pl.multiple_of(my_y * slab, slab), slab)]
+        total = total + r1[my_x, my_y].astype(F32)
+        for to in xy_order[::-1]:
+            xy_scatter(*to).wait_recv()
+            total = total + r2[to[0] * ny + to[1]].astype(F32)
+        zall[my_z] = total.astype(BF)
+        start([z_spread(d) for d in sorted(range(1, nz), key=lambda d: -min(d, nz - d))])
 
     def reduce_z():
-        arrive(every(z_scatter, nz))
-        r4[my_z] = (s3[my_z] + jnp.sum(r3[...], axis=0)) * scaling
-        start(every(z_gather, nz))
-
-    def gather_z():
-        arrive(every(z_gather, nz))
-        for i in range(nz):
-            rowtmp[pl.ds(i * piece, piece)] = r4[i]
-        gfull[my_core, my_x, my_y] = rowtmp[...].astype(BF)
-        start(every(y_gather, ny))
-
-    def gather_y():
-        arrive(every(y_gather, ny))
-        start([x_gather(d) for d in far_first])
-        core_gather(0).start()
-
-    def gather_x():
-        for d in near_first:
-            x_gather(d).wait_recv()
-            core_gather(d).start()
-        for d in range(nx):
-            core_gather(d).wait_recv()
+        arrive([z_spread(d) for d in range(1, nz)])
+        total = zall[0].astype(F32)
+        for z in range(1, nz):
+            total = total + zall[z].astype(F32)
+        gfull[my_core, my_x, my_y] = (total * scaling).astype(BF)
+        start([xy_gather(*to) for to in xy_order])
+
+    def gather_xy():
+        for dx in near_first:
+            arrive([xy_gather(*to) for to in xy_order if to[0] == dx])
+            core_gather(dx).start()
+
+    def gather_core():
+        arrive([core_gather(d) for d in range(nx)])
 
     def mine(ext, r0, count):
         return ext[pl.ds(r0 + 1, count), pl.ds(0, own)].reshape(count * own, chans)
@@ -494,29 +463,26 @@
         first_back,
         lambda part: weight_grads(part * (rows // 2), rows // 2, part == 0),
     )
-    gb[...] = p32[1 - my_core].astype(BF)
-    start([core_scatter(d) for d in far_first + [0]])
+    gb[...] = p32[1 - my_core].astype(BF).reshape(gb.shape)
+    start([core_scatter(d) for d in far_first])
     reduce_core()
+    halves(2, ext_h, second)
+    reduce_xy()
     sent(halo(2, ext_h))
     start(halo(3, ext_d))
-
-    halves(2, ext_h, second)
     emit(0, out_ref)
-    reduce_x()
-    reduce_y()
-    halves(3, ext_d, second_back, lambda part: reduce_z() if part == 0 else None)
-    gather_z()
+    reduce_z()
+    halves(3, ext_d, second_back)
     emit(1, gin_ref)
-    gather_y()
-    gather_x()
+    gather_xy()
+    gather_core()
     last = pltpu.make_async_copy(gfull, grad_ref, out_sem.at[2])
     last.start()
 
     sent(halo(3, ext_d) + tap_copies())
     sent([make(d) for make in (core_scatter, core_gather) for d in range(nx)])
-    sent(every(x_scatter, nx) + every(x_gather, nx))
-    sent(every(y_scatter, ny) + every(y_gather, ny))
-    sent(every(z_scatter, nz) + every(z_gather, nz))
+    sent([make(*to) for make in (xy_scatter, xy_gather) for to in xy_order])
+    sent([z_spread(d) for d in range(1, nz)])
     outgoing(0, out_ref).wait()
     outgoing(1, gin_ref).wait()
     last.wait()
@@ -570,7 +536,6 @@
     own = -(-cols // 16) * 16
     chunk = count * chans // nx
     slab = chunk // ny
-    piece = slab // nz
 
     vmem = pl.BlockSpec(memory_space=pltpu.VMEM)
     smem = pl.BlockSpec(memory_space=pltpu.SMEM)
@@ -609,17 +574,11 @@
             pltpu.VMEM((2, rows, own, chans), BF),
             pltpu.VMEM((2, own, rows, chans), BF),
             pltpu.VMEM((2, nx, chunk, chans), F32),
-            pltpu.VMEM((nx, chunk, chans), BF),
-            pltpu.VMEM((nx, chunk, chans), BF),
-            pltpu.VMEM((nx, chunk, chans), BF),
-            pltpu.VMEM((nx - 1, chunk, chans), BF),
-            pltpu.VMEM((ny, slab, chans), F32),
-            pltpu.VMEM((ny, slab, chans), BF),
-            pltpu.VMEM((ny - 1, slab, chans), BF),
-            pltpu.VMEM((nz, piece, chans), F32),
-            pltpu.VMEM((nz - 1, piece, chans), F32),
-            pltpu.VMEM((nz, piece, chans), F32),
-            pltpu.VMEM((slab, chans), F32),
+            pltpu.VMEM((nx, ny, slab, chans), BF),
+            pltpu.VMEM((nx, ny, slab, chans), BF),
+            pltpu.VMEM((nx, ny, slab, chans), BF),
+            pltpu.VMEM((nx * ny, slab, chans), BF),
+            pltpu.VMEM((nz, slab, chans), BF),
             pltpu.VMEM((2, nx, ny, slab, chans), BF),
             dma((4,)),
             dma((3,)),
@@ -629,12 +588,10 @@
             dma((2,)),
             dma((2, nx)),
             dma((2, nx)),
-            dma((2, nx)),
-            dma((2, nx)),
-            dma((2, ny)),
-            dma((2, ny)),
-            dma((2, nz)),
-            dma((2, nz)),
+            dma((2, nx * ny)),
+            dma((2, nx * ny)),
+            dma((nz,)),
+            dma((nz,)),
         ],
         compiler_params=pltpu.CompilerParams(
             collective_id=0, has_side_effects=True, vmem_limit_bytes=60 * 1024 * 1024

time: 72.4 us -> 65.3 us (0.902)
  Pallas kernels: 71.6 us -> 64.5 us
    pallas_call x1, Pallas kernels: 68.7 us -> 61.6 us  [local(): pl.pallas_call(functools.partial(kernel, (nx, nyl, nz, nyh, rows, cols, c...]
where the time goes in v3:
time: 65.3 us; the launch traced here: 65.1 us
  Pallas kernels  64.5 us (99%)
    pallas_call x1, Pallas kernels, local(): pl.pallas_call(functools.partial(kernel, (nx, nyl, nz, nyh, rows, cols, c...  61.6 us
    pallas_call x1, Pallas kernels, local(): pl.pallas_call(functools.partial(deliver, nx, chunk // 2), out_shape=(fie...  2.9 us

profile of v3, /device:TPU:1, one launch (start us, length us, event | category | flops | bytes accessed | tf_op | source)
XLA Modules:
  0.0 65.1 jit_solution(9347184300683057689)
XLA Ops:
  0.6 61.6 %shard_map.93 = (bf16[90,16,256]{2,1,0:T(8,128)(2,1)}, bf16[90,16,256]{2,1,0:T(8,128)(2,1)}, bf16[2,4,4,48,256]{4,3,2,1,0:T(8,128)(2,1)}) custom-call(bf16[90,16,256]{2,1,0:T(8,128)(2,1)} %bitcast.7, bf16[90,16,256]{2,1,0:T(8,128)(2,1)} %bitcast.8, bf16[3,3,16,33]{3,2,1,0:T(8,128)(2,1)} %bitcast.9, s32[16]{0:T(128)} %support_ref.1, ...), custom_call_target="tpu_custom_call" | custom-call | tf_op jit(solution)/shard_map/pallas_call | solution.py:546
  62.2 2.9 %shard_map.94 = (bf16[90,16,256]{2,1,0:T(8,128)(2,1)}, bf16[90,16,256]{2,1,0:T(8,128)(2,1)}, f32[768,256]{1,0:T(8,128)}, f32[768,256]{1,0:T(8,128)}) custom-call(bf16[90,16,256]{2,1,0:T(8,128)(2,1)} %get-tuple-element.11.out_in, bf16[90,16,256]{2,1,0:T(8,128)(2,1)} %get-tuple-element.12.gin_in, bf16[2,4,4,48,256]{4,3,2,1,0:T(8,128)(2,1)} %get-tuple-element.13.grad_in), custom_call_target="tpu_custom_call" | custom-call | tf_op jit(solution)/shard_map/pallas_call | solution.py:608

commit v4 on v3

--- a/solution.py
+++ b/solution.py
@@ -488,42 +488,27 @@
     last.wait()
 
 
-def deliver(nx, half, out_in, gin_in, grad_in, out_ref, gin_ref, g1_ref, g2_ref, *scratch):
-    out, gin, grad, g1, g2, in_sems, out_sems = scratch
-    cells = out.shape[0]
-    cut = cells // 2
-
-    def put(i, src, dst, sems):
+def deliver(nx, half, out_in, gin_in, grad_in, out_ref, gin_ref, g1_ref, g2_ref, grad, g1, g2, sems):
+    def put(i, src, dst):
         return pltpu.make_async_copy(src, dst, sems.at[i])
 
-    steps = [(4, grad_in, grad)]
-    for i, (src, dst) in enumerate([(out_in, out), (gin_in, gin)]):
-        steps += [(2 * i + j, src.at[at], dst.at[at]) for j, at in enumerate(parts_of(cells, cut))]
-    arriving = [put(i, src, dst, in_sems) for i, src, dst in steps]
-    for copy in arriving:
+    arriving = put(4, grad_in, grad)
+    arriving.start()
+    leaving = [put(0, out_in, out_ref), put(1, gin_in, gin_ref)]
+    for copy in leaving:
         copy.start()
-    arriving[0].wait()
+    arriving.wait()
     for core in range(2):
         for x in range(nx):
             at = pl.ds((core * nx + x) * half, half)
             flat = grad[core, x].reshape(2 * half, grad.shape[-1]).astype(F32)
             g1[at] = flat[:half]
             g2[at] = flat[half:]
-    leaving = [put(4, g1, g1_ref, out_sems), put(5, g2, g2_ref, out_sems)]
-    for copy in leaving:
+    leaving += [put(2, g1, g1_ref), put(3, g2, g2_ref)]
+    for copy in leaving[2:]:
         copy.start()
-    for i, (src, dst) in enumerate([(out, out_ref), (gin, gin_ref)]):
-        for j, at in enumerate(parts_of(cells, cut)):
-            arriving[1 + 2 * i + j].wait()
-            copy = put(2 * i + j, src.at[at], dst.at[at], out_sems)
-            copy.start()
-            leaving.append(copy)
     for copy in leaving:
         copy.wait()
-
-
-def parts_of(count, cut):
-    return pl.ds(0, cut), pl.ds(cut, count - cut)
 
 
 def local(sizes, features, cotangent, basis, support, weight_one, weight_two):
@@ -545,7 +530,11 @@
     field = jax.ShapeDtypeStruct((cols, rows, chans), BF)
     out, gin, grads = pl.pallas_call(
         functools.partial(kernel, (nx, nyl, nz, nyh, rows, cols, chans, count, scaling)),
-        out_shape=(field, field, jax.ShapeDtypeStruct((2, nx, ny, slab, chans), BF)),
+        out_shape=(
+            pltpu.VMEM((cols, rows, chans), BF),
+            pltpu.VMEM((cols, rows, chans), BF),
+            pltpu.VMEM((2, nx, ny, slab, chans), BF),
+        ),
         in_specs=[hbm, hbm, vmem, smem, hbm, hbm],
         out_specs=(hbm,) * 3,
         scratch_shapes=[
@@ -594,7 +583,7 @@
             dma((nz,)),
         ],
         compiler_params=pltpu.CompilerParams(
-            collective_id=0, has_side_effects=True, vmem_limit_bytes=60 * 1024 * 1024
+            collective_id=0, has_side_effects=True, vmem_limit_bytes=58 * 1024 * 1024
         ),
     )(
         features.transpose(1, 0, 2),
@@ -611,15 +600,12 @@
         in_specs=[hbm] * 3,
         out_specs=(hbm,) * 4,
         scratch_shapes=[
-            pltpu.VMEM(field.shape, BF),
-            pltpu.VMEM(field.shape, BF),
             pltpu.VMEM(grads.shape, BF),
             pltpu.VMEM(weights.shape, F32),
             pltpu.VMEM(weights.shape, F32),
             dma((5,)),
-            dma((6,)),
         ],
-        compiler_params=pltpu.CompilerParams(vmem_limit_bytes=60 * 1024 * 1024),
+        compiler_params=pltpu.CompilerParams(vmem_limit_bytes=8 * 1024 * 1024),
     )(out, gin, grads)
     shape = weight_one.shape
     return out.transpose(1, 0, 2), gin.transpose(1, 0, 2), g1.reshape(shape), g2.reshape(shape)

time: 65.3 us -> 63.4 us (0.971)
  Pallas kernels: 64.5 us -> 62.6 us
    pallas_call x1, Pallas kernels: 2.9 us -> 1.72 us  [local(): pl.pallas_call(functools.partial(deliver, nx, chunk // 2), out_shape=(fie...]
    pallas_call x1, Pallas kernels: 61.6 us -> 60.8 us  [local(): pl.pallas_call(functools.partial(kernel, (nx, nyl, nz, nyh, rows, cols, c...]
where the time goes in v4:
time: 63.4 us; the launch traced here: 63.2 us
  Pallas kernels  62.6 us (99%)
  between operations  0.64 us (1%)
    pallas_call x1, Pallas kernels, local(): pl.pallas_call(functools.partial(kernel, (nx, nyl, nz, nyh, rows, cols, c...  60.8 us
    pallas_call x1, Pallas kernels, local(): pl.pallas_call(functools.partial(deliver, nx, chunk // 2), out_shape=(fie...  1.72 us

profile of v4, /device:TPU:1, one launch (start us, length us, event | category | flops | bytes accessed | tf_op | source)
XLA Modules:
  0.0 63.2 jit_solution(14836718654217883759)
XLA Ops:
  0.6 60.8 %shard_map.93 = (bf16[90,16,256]{2,1,0:T(8,128)(2,1)S(1)}, bf16[90,16,256]{2,1,0:T(8,128)(2,1)S(1)}, bf16[2,4,4,48,256]{4,3,2,1,0:T(8,128)(2,1)S(1)}) custom-call(bf16[90,16,256]{2,1,0:T(8,128)(2,1)} %bitcast.7, bf16[90,16,256]{2,1,0:T(8,128)(2,1)} %bitcast.8, bf16[3,3,16,33]{3,2,1,0:T(8,128)(2,1)} %bitcast.9, s32[16]{0:T(128)} %support_ref.1, ...), custom_call_target="tpu_custom_call" | custom-call | tf_op jit(solution)/shard_map/pallas_call | solution.py:531
  61.5 1.7 %shard_map.94 = (bf16[90,16,256]{2,1,0:T(8,128)(2,1)}, bf16[90,16,256]{2,1,0:T(8,128)(2,1)}, f32[768,256]{1,0:T(8,128)}, f32[768,256]{1,0:T(8,128)}) custom-call(bf16[90,16,256]{2,1,0:T(8,128)(2,1)S(1)} %get-tuple-element.11.out_in, bf16[90,16,256]{2,1,0:T(8,128)(2,1)S(1)} %get-tuple-element.12.gin_in, bf16[2,4,4,48,256]{4,3,2,1,0:T(8,128)(2,1)S(1)} %get-tuple-element.13.grad_in), custom_call_target="tpu_custom_call" | custom-call | tf_op jit(solution)/shard_map/pallas_call | solution.py:597

commit v5 on v4

--- a/solution.py
+++ b/solution.py
@@ -88,7 +88,7 @@
     left = WIDE - HW
     nlat, nlon = nx * nyl * 2, nz * nyh
     ny = nyl * nyh
-    blk = 4
+    blk = 8
     nblk = rows // blk
     wide_chans = basis * chans
 
@@ -163,10 +163,13 @@
     def turn(block):
         return dot(perm[...], block.reshape(side, chans)).astype(BF).reshape(HW, HW, chans)
 
-    def stage(field, raw, ext):
+    def stage_ends(field, raw, ext):
+        tails[field] = turn(raw[pl.ds(cols - HW, HW)])
+        ext[pl.ds(1, rows), pl.ds(0, HW)] = turn(raw[pl.ds(0, HW)])
+
+    def stage_rest(raw, ext):
         raw[pl.ds(cols, own - cols)] = jnp.zeros((own - cols, rows, chans), BF)
-        tails[field] = turn(raw[pl.ds(cols - HW, HW)])
-        for b in range(own // HW):
+        for b in range(1, own // HW):
             ext[pl.ds(1, rows), pl.ds(b * HW, HW)] = turn(raw[pl.ds(b * HW, HW)])
 
     def remote(src, dst, snd, rcv, device):
@@ -224,9 +227,13 @@
             copy.wait_send()
 
     inputs[0].wait()
-    stage(0, raw_f, ext_f)
+    stage_ends(0, raw_f, ext_f)
     pl.semaphore_wait(barrier, len(around) + len(others))
-    start(halo(0, ext_f))
+    margins = halo(0, ext_f)
+    whole_rows = margins[2::5]
+    start([copy for i, copy in enumerate(margins) if i % 5 != 2])
+    stage_rest(raw_f, ext_f)
+    start(whole_rows)
 
     loose[...] = jnp.zeros(loose.shape, F32)
     row = iota((rows, WIDE), 0)
@@ -294,7 +301,8 @@
     lax.fori_loop(0, rows, build_fwd, 0)
 
     inputs[1].wait()
-    stage(1, raw_c, ext_c)
+    stage_ends(1, raw_c, ext_c)
+    stage_rest(raw_c, ext_c)
     inputs[2].wait()
     inputs[3].wait()
     eye = jnp.where(iota((chans, chans), 0) == iota((chans, chans), 1), 1.0, 0.0).astype(BF)
@@ -463,8 +471,10 @@
         first_back,
         lambda part: weight_grads(part * (rows // 2), rows // 2, part == 0),
     )
-    gb[...] = p32[1 - my_core].astype(BF).reshape(gb.shape)
-    start([core_scatter(d) for d in far_first])
+    for d in far_first:
+        x = x_peers[d]
+        gb[x] = p32[1 - my_core, x].astype(BF).reshape(ny, slab, chans)
+        core_scatter(d).start()
     reduce_core()
     halves(2, ext_h, second)
     reduce_xy()

time: 63.4 us -> 63.5 us (level)
  no operation moved by 1% of the time
where the time goes in v5:
time: 63.5 us; the launch traced here: 63.3 us
  Pallas kernels  62.7 us (99%)
  between operations  0.64 us (1%)
    pallas_call x1, Pallas kernels, local(): pl.pallas_call(functools.partial(kernel, (nx, nyl, nz, nyh, rows, cols, c...  61 us
    pallas_call x1, Pallas kernels, local(): pl.pallas_call(functools.partial(deliver, nx, chunk // 2), out_shape=(fie...  1.72 us

profile of v5, /device:TPU:1, one launch (start us, length us, event | category | flops | bytes accessed | tf_op | source)
XLA Modules:
  0.0 63.3 jit_solution(3325246995528955875)
XLA Ops:
  0.6 61.0 %shard_map.93 = (bf16[90,16,256]{2,1,0:T(8,128)(2,1)S(1)}, bf16[90,16,256]{2,1,0:T(8,128)(2,1)S(1)}, bf16[2,4,4,48,256]{4,3,2,1,0:T(8,128)(2,1)S(1)}) custom-call(bf16[90,16,256]{2,1,0:T(8,128)(2,1)} %bitcast.7, bf16[90,16,256]{2,1,0:T(8,128)(2,1)} %bitcast.8, bf16[3,3,16,33]{3,2,1,0:T(8,128)(2,1)} %bitcast.9, s32[16]{0:T(128)} %support_ref.1, ...), custom_call_target="tpu_custom_call" | custom-call | tf_op jit(solution)/shard_map/pallas_call | solution.py:541
  61.6 1.7 %shard_map.94 = (bf16[90,16,256]{2,1,0:T(8,128)(2,1)}, bf16[90,16,256]{2,1,0:T(8,128)(2,1)}, f32[768,256]{1,0:T(8,128)}, f32[768,256]{1,0:T(8,128)}) custom-call(bf16[90,16,256]{2,1,0:T(8,128)(2,1)S(1)} %get-tuple-element.11.out_in, bf16[90,16,256]{2,1,0:T(8,128)(2,1)S(1)} %get-tuple-element.12.gin_in, bf16[2,4,4,48,256]{4,3,2,1,0:T(8,128)(2,1)S(1)} %get-tuple-element.13.grad_in), custom_call_target="tpu_custom_call" | custom-call | tf_op jit(solution)/shard_map/pallas_call | solution.py:607
